TPU v7x, 32 devices: a whole 2x2x4 slice. The times are simulated.
32 devices in a mesh: frame: 16 (over z, y, core), seq: 2 (over x).
Axes of the slice: x: 2, y: 2, z: 4, core: 2. Of those that a mesh axis runs over, the one named last changes fastest.
Arguments:
- tokens: bfloat16 [4, 3136, 384], P('seq', 'frame'), may hold values from -6 to 6
- segments: int32 [4, 3136], P('seq', 'frame'), may hold values from 0 to 3, as said below
- g_attn: float32 [384], replicated, may hold values from 0.1 to 1.9
- w_qkv: bfloat16 [384, 1152], replicated, may hold values from -0.3125 to 0.3125
- w_out: bfloat16 [384, 384], replicated, may hold values from -6 to 6
- g_mlp: float32 [384], replicated, may hold values from 0.1 to 1.9
- w_up: bfloat16 [384, 1536], replicated, may hold values from -0.3125 to 0.3125
- w_down: bfloat16 [1536, 384], replicated, may hold values from -0.15625 to 0.15625
- g_learn: float32 [384], replicated, may hold values from 0.1 to 1.9
- conv_first: bfloat16 [8, 3, 3, 384], replicated, may hold values from -0.109375 to 0.109375
- conv_rest: bfloat16 [3, 8, 3, 3, 8], replicated, may hold values from -0.75 to 0.75
- d_learned: bfloat16 [4, 128, 384], P('seq', 'frame'), may hold values from -6 to 6
Outputs:
- learned: bfloat16 [4, 128, 384], P('seq', 'frame')
- d_tokens: float32 [4, 3136, 384], P('seq', 'frame')
- d_g_attn: float32 [384], replicated
- d_w_qkv: float32 [384, 1152], replicated
- d_w_out: float32 [384, 384], replicated
- d_g_mlp: float32 [384], replicated
- d_w_up: float32 [384, 1536], replicated
- d_w_down: float32 [1536, 384], replicated
- d_g_learn: float32 [384], replicated
- d_conv_first: float32 [8, 3, 3, 384], replicated
- d_conv_rest: float32 [3, 8, 3, 3, 8], replicated
Inputs may be any that keep to these rules, and one draw needn't show every extreme that they name: `segments`: within a sequence the clip numbers never fall, are equal on all 196 tokens of a frame and start at 0; a sequence is one clip (all 0) or four clips of whole frames; among the 2 sequences of each index of seq at least one is one clip and at least one holds four.
All inputs are finite; a program needn't handle non-finite values.
Results may differ from a plain program's by a relative error of at most 0.019.
Values may be sent and summed in bfloat16 or wider, within the bound.
A program may use at most 192 MiB of HBM per device.

v0:
```python
import math

import jax
import jax.numpy as jnp
from jax import lax
from jax.sharding import PartitionSpec as P

HEADS = 6
HEAD_DIM = 64
MAPS = 8
GRID = 14


def layer_norm(values, gain):
    average = jnp.mean(values, axis=-1, keepdims=True)
    centered = values - average
    variance = jnp.mean(centered * centered, axis=-1, keepdims=True)
    return centered * lax.rsqrt(variance + 1e-06) * gain


def gelu_tanh(values):
    return (
        0.5
        * values
        * (1.0 + jnp.tanh(0.7978845608028654 * (values + 0.044715 * values * values * values)))
    )


def conv_small(field, weight):
    grid_side = field.shape[1]
    padded = jnp.pad(field, ((0, 0), (1, 1), (1, 1), (0, 0)))
    result = jnp.zeros(field.shape[:3] + (weight.shape[0],), jnp.float32)
    for shift_row in range(3):
        for shift_col in range(3):
            window = padded[
                :, shift_row : shift_row + grid_side, shift_col : shift_col + grid_side, :
            ]
            result = result + jnp.einsum(
                "fxyc,oc->fxyo",
                window,
                weight[:, shift_row, shift_col, :],
                precision=lax.Precision.HIGHEST,
            )
    return result


def map_tail(first_out, conv_rest, frames):
    current = first_out
    for layer_idx in range(3):
        current = conv_small(gelu_tanh(current), conv_rest[layer_idx])
    map_weights = 1.0 / (1.0 + jnp.exp(-current))
    cell_count = frames.shape[1] * frames.shape[2]
    pooled = (
        jnp.einsum("fxym,fxyd->fmd", map_weights, frames, precision=lax.Precision.HIGHEST)
        / cell_count
    )
    return pooled.reshape(-1, frames.shape[3])


def conv_first_apply(field, weight):
    grid_side = field.shape[1]
    padded = jnp.pad(field, ((0, 0), (1, 1), (1, 1), (0, 0)))
    taps = weight.reshape(weight.shape[0], 9, weight.shape[3])
    projected = jnp.einsum("sxyc,otc->sxyot", padded, taps, preferred_element_type=jnp.float32)
    result = jnp.zeros(field.shape[:3] + (weight.shape[0],), jnp.float32)
    for shift_row in range(3):
        for shift_col in range(3):
            result = (
                result
                + projected[
                    :,
                    shift_row : shift_row + grid_side,
                    shift_col : shift_col + grid_side,
                    :,
                    3 * shift_row + shift_col,
                ]
            )
    return result


def spread_taps(grad_map):
    shifted = [
        jnp.pad(grad_map, ((0, 0), (shift_row, 2 - shift_row), (shift_col, 2 - shift_col), (0, 0)))
        for shift_row in range(3)
        for shift_col in range(3)
    ]
    return jnp.stack(shifted, axis=-1)


def bounded(fold_fn, limit, carry, pieces):
    span = pieces[0].shape[1]
    block_len = min(span, limit)
    block_count = span // block_len

    def one_block(block_idx, state):
        offset = block_idx * block_len
        sub_pieces = tuple(
            (lax.dynamic_slice_in_dim(piece, offset, block_len, 1) for piece in pieces)
        )
        return fold_fn(state, sub_pieces, offset)

    return lax.fori_loop(0, block_count, one_block, carry)


def on_device(
    tokens,
    segments,
    g_attn,
    w_qkv,
    w_out,
    g_mlp,
    w_up,
    w_down,
    g_learn,
    conv_first,
    conv_rest,
    d_learned,
):
    seq_count, frame_rows, width = tokens.shape
    row_count = seq_count * frame_rows
    scale_qk = HEAD_DIM ** (-0.5)
    limit_rows = 4 * frame_rows
    inputs = tokens.astype(jnp.float32).reshape(row_count, width)
    hidden_one, norm_one_back = jax.vjp(layer_norm, inputs, g_attn)
    hidden_one_bf = hidden_one.astype(jnp.bfloat16)
    projected = jnp.dot(hidden_one_bf, w_qkv, preferred_element_type=jnp.float32).astype(
        jnp.bfloat16
    )
    query_flat = projected[:, :width].reshape(seq_count, frame_rows, width)
    queries = query_flat.reshape(seq_count, frame_rows, HEADS, HEAD_DIM)
    key_rows = projected[:, width : 2 * width].reshape(seq_count, frame_rows, width)
    value_rows = projected[:, 2 * width :].reshape(seq_count, frame_rows, width)
    own_keys = key_rows.reshape(seq_count, frame_rows, HEADS, HEAD_DIM)
    own_values = value_rows.reshape(seq_count, frame_rows, HEADS, HEAD_DIM)
    all_segments = lax.all_gather(segments, "frame", axis=1, tiled=True)

    def forward_block(carry, pieces, start):
        attn_acc, running_max, running_sum = carry
        span = pieces[0].shape[1]
        key_heads = pieces[0].reshape(seq_count, span, HEADS, HEAD_DIM)
        value_heads = pieces[1].reshape(seq_count, span, HEADS, HEAD_DIM)
        key_seg = lax.dynamic_slice_in_dim(all_segments, start, span, 1)
        allowed = segments[:, :, None] == key_seg[:, None, :]
        scores = (
            jnp.einsum("sqhd,skhd->shqk", queries, key_heads, preferred_element_type=jnp.float32)
            * scale_qk
        )
        scores = jnp.where(allowed[:, None], scores, -1e30)
        new_max = jnp.maximum(running_max, jnp.max(scores, axis=-1))
        rescale = jnp.exp(running_max - new_max)
        expon = jnp.exp(scores - new_max[..., None])
        running_sum = running_sum * rescale + jnp.sum(expon, axis=-1)
        attn_acc = attn_acc * rescale[..., None] + jnp.einsum(
            "shqk,skhd->shqd",
            expon.astype(jnp.bfloat16),
            value_heads,
            preferred_element_type=jnp.float32,
        )
        return (attn_acc, new_max, running_sum)

    start_state = (
        jnp.zeros((seq_count, HEADS, frame_rows, HEAD_DIM), jnp.float32),
        jnp.full((seq_count, HEADS, frame_rows), -1e30, jnp.float32),
        jnp.zeros((seq_count, HEADS, frame_rows), jnp.float32),
    )
    attn_acc, running_max, running_sum = bounded(
        forward_block,
        limit_rows,
        start_state,
        (
            lax.all_gather(key_rows, "frame", axis=1, tiled=True),
            lax.all_gather(value_rows, "frame", axis=1, tiled=True),
        ),
    )
    mixed = attn_acc / running_sum[..., None]
    log_total = running_max + jnp.log(running_sum)
    attended = mixed.transpose(0, 2, 1, 3).reshape(row_count, width).astype(jnp.bfloat16)
    after_attn = inputs + jnp.dot(attended, w_out, preferred_element_type=jnp.float32)
    hidden_two, norm_two_back = jax.vjp(layer_norm, after_attn, g_mlp)
    hidden_two_bf = hidden_two.astype(jnp.bfloat16)
    pre_act = jnp.dot(hidden_two_bf, w_up, preferred_element_type=jnp.float32)
    activated, gelu_back = jax.vjp(gelu_tanh, pre_act)
    activated_bf = activated.astype(jnp.bfloat16)
    block_out = after_attn + jnp.dot(activated_bf, w_down, preferred_element_type=jnp.float32)
    frames = block_out.reshape(seq_count, GRID, GRID, width)
    hidden_three, norm_three_back = jax.vjp(layer_norm, frames, g_learn)
    hidden_three_bf = hidden_three.astype(jnp.bfloat16)
    first_out = conv_first_apply(hidden_three_bf, conv_first)
    pooled, tail_back = jax.vjp(map_tail, first_out, conv_rest.astype(jnp.float32), frames)
    learned = pooled.astype(jnp.bfloat16).reshape(seq_count, MAPS, width)
    d_first, d_rest, d_frames_pool = tail_back(
        d_learned.astype(jnp.float32).reshape(seq_count * MAPS, width)
    )
    spread = spread_taps(d_first.astype(jnp.bfloat16))
    padded_three = jnp.pad(hidden_three_bf, ((0, 0), (1, 1), (1, 1), (0, 0)))
    first_taps = conv_first.reshape(MAPS, 9, width)
    d_conv_first = jnp.einsum(
        "sxyc,sxyot->otc", padded_three, spread, preferred_element_type=jnp.float32
    ).reshape(MAPS, 3, 3, width)
    d_padded = jnp.einsum("sxyot,otc->sxyc", spread, first_taps, preferred_element_type=jnp.float32)
    d_hidden_three = d_padded[:, 1 : 1 + GRID, 1 : 1 + GRID, :]
    d_frames_norm, d_g_learn = norm_three_back(d_hidden_three)
    d_block = (d_frames_pool + d_frames_norm).reshape(row_count, width)
    d_branch = d_block.astype(jnp.bfloat16)
    d_w_down = jnp.einsum("nf,nd->fd", activated_bf, d_branch, preferred_element_type=jnp.float32)
    d_activated = jnp.einsum("nd,fd->nf", d_branch, w_down, preferred_element_type=jnp.float32)
    d_pre = gelu_back(d_activated)[0].astype(jnp.bfloat16)
    d_w_up = jnp.einsum("nd,nf->df", hidden_two_bf, d_pre, preferred_element_type=jnp.float32)
    d_hidden_two = jnp.einsum("nf,df->nd", d_pre, w_up, preferred_element_type=jnp.float32)
    d_after_norm, d_g_mlp = norm_two_back(d_hidden_two)
    d_after = d_block + d_after_norm
    d_attn_branch = d_after.astype(jnp.bfloat16)
    d_w_out = jnp.einsum("nd,ne->de", attended, d_attn_branch, preferred_element_type=jnp.float32)
    d_attended = jnp.einsum(
        "ne,de->nd", d_attn_branch, w_out, preferred_element_type=jnp.float32
    ).astype(jnp.bfloat16)
    d_flat = d_attended.reshape(seq_count, frame_rows, width)
    d_heads = d_attended.reshape(seq_count, frame_rows, HEADS, HEAD_DIM)
    delta_row = jnp.sum(d_heads.astype(jnp.float32).transpose(0, 2, 1, 3) * mixed, axis=-1)
    empty_grad = jnp.zeros((seq_count, frame_rows, HEADS, HEAD_DIM), jnp.float32)

    def query_grad_block(grad_q, pieces, start):
        span = pieces[0].shape[1]
        key_heads = pieces[0].reshape(seq_count, span, HEADS, HEAD_DIM)
        value_heads = pieces[1].reshape(seq_count, span, HEADS, HEAD_DIM)
        key_seg = lax.dynamic_slice_in_dim(all_segments, start, span, 1)
        allowed = segments[:, :, None] == key_seg[:, None, :]
        scores = (
            jnp.einsum("sqhd,skhd->shqk", queries, key_heads, preferred_element_type=jnp.float32)
            * scale_qk
        )
        scores = jnp.where(allowed[:, None], scores, -1e30)
        attn_prob = jnp.exp(scores - log_total[..., None])
        d_prob = jnp.einsum(
            "sqhd,skhd->shqk", d_heads, value_heads, preferred_element_type=jnp.float32
        )
        d_scores = (attn_prob * (d_prob - delta_row[..., None])).astype(jnp.bfloat16)
        return (
            grad_q
            + jnp.einsum("shqk,skhd->sqhd", d_scores, key_heads, preferred_element_type=jnp.float32)
            * scale_qk
        )

    grad_q = bounded(
        query_grad_block,
        limit_rows,
        empty_grad,
        (
            lax.all_gather(key_rows, "frame", axis=1, tiled=True),
            lax.all_gather(value_rows, "frame", axis=1, tiled=True),
        ),
    )
    log_all, delta_all = (
        lax.all_gather(log_total, "frame", axis=2, tiled=True),
        lax.all_gather(delta_row, "frame", axis=2, tiled=True),
    )

    def key_grad_block(carry, pieces, start):
        grad_k, grad_v = carry
        span = pieces[0].shape[1]
        query_heads = pieces[0].reshape(seq_count, span, HEADS, HEAD_DIM)
        grad_heads = pieces[1].reshape(seq_count, span, HEADS, HEAD_DIM)
        query_seg = lax.dynamic_slice_in_dim(all_segments, start, span, 1)
        allowed = query_seg[:, :, None] == segments[:, None, :]
        scores = (
            jnp.einsum("sqhd,skhd->shqk", query_heads, own_keys, preferred_element_type=jnp.float32)
            * scale_qk
        )
        scores = jnp.where(allowed[:, None], scores, -1e30)
        piece_log = lax.dynamic_slice_in_dim(log_all, start, span, 2)
        piece_delta = lax.dynamic_slice_in_dim(delta_all, start, span, 2)
        attn_prob = jnp.exp(scores - piece_log[..., None])
        d_prob = jnp.einsum(
            "sqhd,skhd->shqk", grad_heads, own_values, preferred_element_type=jnp.float32
        )
        d_scores = (attn_prob * (d_prob - piece_delta[..., None])).astype(jnp.bfloat16)
        grad_k = (
            grad_k
            + jnp.einsum(
                "shqk,sqhd->skhd", d_scores, query_heads, preferred_element_type=jnp.float32
            )
            * scale_qk
        )
        grad_v = grad_v + jnp.einsum(
            "shqk,sqhd->skhd",
            attn_prob.astype(jnp.bfloat16),
            grad_heads,
            preferred_element_type=jnp.float32,
        )
        return (grad_k, grad_v)

    grad_k, grad_v = bounded(
        key_grad_block,
        limit_rows,
        (empty_grad, empty_grad),
        (
            lax.all_gather(query_flat, "frame", axis=1, tiled=True),
            lax.all_gather(d_flat, "frame", axis=1, tiled=True),
        ),
    )
    d_projected = jnp.concatenate(
        [
            grad_q.reshape(row_count, width),
            grad_k.reshape(row_count, width),
            grad_v.reshape(row_count, width),
        ],
        axis=1,
    ).astype(jnp.bfloat16)
    d_w_qkv = jnp.einsum(
        "nd,ne->de", hidden_one_bf, d_projected, preferred_element_type=jnp.float32
    )
    d_hidden_one = jnp.einsum("ne,de->nd", d_projected, w_qkv, preferred_element_type=jnp.float32)
    d_inputs_norm, d_g_attn = norm_one_back(d_hidden_one)
    d_tokens = (d_after + d_inputs_norm).reshape(seq_count, frame_rows, width)
    small_sums = lax.psum((d_g_attn, d_g_mlp, d_g_learn, d_conv_first, d_rest), ("frame", "seq"))
    grad_list = [d_w_qkv, d_w_out, d_w_up, d_w_down]
    flat_grads = jnp.concatenate([part_grad.reshape(-1) for part_grad in grad_list])
    share = lax.psum_scatter(flat_grads, ("frame", "seq"), scatter_dimension=0, tiled=True)
    summed = lax.all_gather(share, ("frame", "seq"), axis=0, tiled=True)
    results = []
    position = 0
    for part_grad in grad_list:
        entry_count = math.prod(part_grad.shape)
        results.append(summed[position : position + entry_count].reshape(part_grad.shape))
        position = position + entry_count
    return (
        learned,
        d_tokens,
        small_sums[0],
        results[0],
        results[1],
        small_sums[1],
        results[2],
        results[3],
        small_sums[2],
        small_sums[3],
        small_sums[4],
    )


def solution(mesh):
    in_specs = (
        P("seq", "frame", None),
        P("seq", "frame"),
        P(),
        P(),
        P(),
        P(),
        P(),
        P(),
        P(),
        P(),
        P(),
        P("seq", "frame", None),
    )
    out_specs = (
        P("seq", "frame", None),
        P("seq", "frame", None),
        P(),
        P(),
        P(),
        P(),
        P(),
        P(),
        P(),
        P(),
        P(),
    )
    return jax.shard_map(
        on_device, mesh=mesh, in_specs=in_specs, out_specs=out_specs, check_vma=False
    )
```

profile of v0, /device:TPU:0, one launch (start us, length us, event | category | flops | bytes accessed | tf_op | source)
XLA Modules:
  0.0 890.3 jit_solution(5713532563798896793)
XLA Ops:
  22.7 23.5 %all-gather = s32[16,196,2]{1,2,0:T(2,128)S(1)} all-gather(s32[1,196,2]{1,2,0:T(2,128)S(1)} %bitcast.763), channel_id=1, replica_groups=mesh['frame'=16,'seq'=2] {'frame'}, dimensions={0}, use_global_device_ids=true | all-gather | bytes 26656 | tf_op jit(solution)/shard_map/all_gather | solution.py:135
  53.2 20.1 %all-gather.7.cloned.1.call-done = bf16[2,3136,384]{2,0,1:T(2,128)(2,1)} async-done(((bf16[2,196,384]{2,0,1:T(2,128)(2,1)}), bf16[2,3136,384]{2,0,1:T(2,128)(2,1)}) %all-gather.7.cloned.1.call-update) | async-done | bytes 4816912 | tf_op jit(solution)/shard_map/all_gather | solution.py:171
  73.2 14.1 %copy.261 = bf16[2,3136,384]{1,2,0:T(8,128)(2,1)} copy(bf16[2,3136,384]{2,0,1:T(2,128)(2,1)} %all-gather.7.cloned.1.call-done) | data formatting | bytes 9633792
  87.4 41.1 %all-gather.9.cloned.1.call-done = bf16[2,3136,384]{2,0,1:T(2,128)(2,1)} async-done(((bf16[2,196,384]{2,0,1:T(2,128)(2,1)}), bf16[2,3136,384]{2,0,1:T(2,128)(2,1)}) %all-gather.9.cloned.1.call-update) | async-done | bytes 4816912 | tf_op jit(solution)/shard_map/all_gather | solution.py:172
  128.5 14.1 %copy.263 = bf16[2,3136,384]{1,2,0:T(8,128)(2,1)} copy(bf16[2,3136,384]{2,0,1:T(2,128)(2,1)} %all-gather.9.cloned.1.call-done) | data formatting | bytes 9633792
  142.6 83.8 %while.48 = (s32[]{:T(128)}, f32[2,6,196,64]{2,3,1,0:T(8,128)}, f32[2,6,196]{2,1,0:T(8,128)S(1)}, f32[2,6,196]{2,1,0:T(8,128)S(1)}, s32[2,196]{1,0:T(2,128)S(1)}...) while((s32[]{:T(128)}, f32[2,6,196,64]{2,3,1,0:T(8,128)}, ...), condition=%wide.region_5.6_spmd.clone, body=%wide.region_2.5_spmd.clone.sunk | while | flops 493110144 | bytes 61762176 | solution.py:102
  147.4 5.1 fusion.337
  152.5 5.4 fusion.338
  168.5 5.1 fusion.337
  173.7 5.4 fusion.338
  179.8 5.0 fusion.340
  189.5 5.1 fusion.337
  194.6 5.4 fusion.338
  200.6 4.9 fusion.340
  210.1 5.1 fusion.337
  215.3 5.4 fusion.338
  221.2 4.9 fusion.340
  275.7 75.8 %while.49 = (s32[]{:T(128)}, f32[2,196,6,64]{1,3,2,0:T(8,128)}, bf16[2,3136,384]{1,2,0:T(8,128)(2,1)}, s32[2,196]{1,0:T(2,128)S(1)}, s32[2,3136]{1,0:T(2,128)S(1...) while((s32[]{:T(128)}, f32[2,196,6,64]{1,3,2,0:T(8,128)}, ...), condition=%wide.region_16.17_spmd.clone, body=%wide.region_15.16_spmd.clone.sunk | while | flops 719906432 | bytes 25641708 | solution.py:102
  280.3 4.9 fusion.347
  285.6 9.1 %fusion.348 = f32[2,196,6,64]{1,3,2,0:T(8,128)} fusion(bf16[2,784,6,64]{1,3,2,0:T(8,128)(2,1)S(1)} %bitcast.756, f32[2,6,784,196]{2,3,1,0:T(8,128)} %fusion.347, f32[2,6,196]{2,1,0:T(8,128)S(1)} %get-tuple-element.1216, f32[2,6,196]{2,1,0:T(8,128)S(1)} %get-tuple-element.1213, pred[2,196,784]{2,1,0:T(8,128)(4,1)S(1)} %broadcast_compare_fusion.7, ...), kind=kOutput, calls=%fused_computation.29.clone.1 | convolution fusion | flops 483571200 | bytes 11615745 | tf_op jit(solution)/shard_map/while/body/eval_jaxpr/shqk,skhd->sqhd/dot_general | solution.py:240
  299.1 4.9 fusion.347
  304.4 9.3 %fusion.348 = f32[2,196,6,64]{1,3,2,0:T(8,128)} fusion(bf16[2,784,6,64]{1,3,2,0:T(8,128)(2,1)S(1)} %bitcast.756, f32[2,6,784,196]{2,3,1,0:T(8,128)} %fusion.347, f32[2,6,196]{2,1,0:T(8,128)S(1)} %get-tuple-element.1216, f32[2,6,196]{2,1,0:T(8,128)S(1)} %get-tuple-element.1213, pred[2,196,784]{2,1,0:T(8,128)(4,1)S(1)} %broadcast_compare_fusion.7, ...), kind=kOutput, calls=%fused_computation.29.clone.1 | convolution fusion | flops 483571200 | bytes 11615745 | tf_op jit(solution)/shard_map/while/body/eval_jaxpr/shqk,skhd->sqhd/dot_general | solution.py:240
  318.1 4.9 fusion.347
  323.3 9.5 %fusion.348 = f32[2,196,6,64]{1,3,2,0:T(8,128)} fusion(bf16[2,784,6,64]{1,3,2,0:T(8,128)(2,1)S(1)} %bitcast.756, f32[2,6,784,196]{2,3,1,0:T(8,128)} %fusion.347, f32[2,6,196]{2,1,0:T(8,128)S(1)} %get-tuple-element.1216, f32[2,6,196]{2,1,0:T(8,128)S(1)} %get-tuple-element.1213, pred[2,196,784]{2,1,0:T(8,128)(4,1)S(1)} %broadcast_compare_fusion.7, ...), kind=kOutput, calls=%fused_computation.29.clone.1 | convolution fusion | flops 483571200 | bytes 11615745 | tf_op jit(solution)/shard_map/while/body/eval_jaxpr/shqk,skhd->sqhd/dot_general | solution.py:240
  337.0 4.9 fusion.347
  342.3 9.3 %fusion.348 = f32[2,196,6,64]{1,3,2,0:T(8,128)} fusion(bf16[2,784,6,64]{1,3,2,0:T(8,128)(2,1)S(1)} %bitcast.756, f32[2,6,784,196]{2,3,1,0:T(8,128)} %fusion.347, f32[2,6,196]{2,1,0:T(8,128)S(1)} %get-tuple-element.1216, f32[2,6,196]{2,1,0:T(8,128)S(1)} %get-tuple-element.1213, pred[2,196,784]{2,1,0:T(8,128)(4,1)S(1)} %broadcast_compare_fusion.7, ...), kind=kOutput, calls=%fused_computation.29.clone.1 | convolution fusion | flops 483571200 | bytes 11615745 | tf_op jit(solution)/shard_map/while/body/eval_jaxpr/shqk,skhd->sqhd/dot_general | solution.py:240
  353.4 42.3 %all_gather.30 = f32[2,6,3136]{1,0,2:T(2,128)} all-gather(f32[2,6,196]{1,0,2:T(2,128)S(1)} %copy-done.36), channel_id=1, replica_groups=mesh['frame'=16,'seq'=2] {'frame'}, dimensions={2}, use_global_device_ids=true | all-gather | bytes 159936 | tf_op jit(solution)/shard_map/all_gather | solution.py:254
  400.5 42.0 %all_gather.32 = f32[2,6,3136]{1,0,2:T(2,128)} all-gather(f32[2,6,196]{1,0,2:T(2,128)S(1)} %copy-done.52), channel_id=1, replica_groups=mesh['frame'=16,'seq'=2] {'frame'}, dimensions={2}, use_global_device_ids=true | all-gather | bytes 159936 | tf_op jit(solution)/shard_map/all_gather | solution.py:255
  465.2 143.1 %while.50 = (s32[]{:T(128)}, f32[2,196,6,64]{1,3,2,0:T(8,128)}, f32[2,196,6,64]{1,3,2,0:T(8,128)}, bf16[2,3136,384]{2,0,1:T(2,128)(2,1)}, s32[2,3136]{1,0:T(2,12...) while((s32[]{:T(128)}, f32[2,196,6,64]{1,3,2,0:T(8,128)}, ...), condition=%wide.region_18.19_spmd.clone, body=%wide.region_17.18_spmd.clone.sunk | while | flops 963611264 | bytes 41999124 | solution.py:102
  473.8 4.9 fusion.356
  480.1 4.8 copy.475
  484.9 9.0 %fusion.357 = f32[2,196,6,64]{1,3,2,0:T(8,128)} fusion(bf16[2,784,6,64]{1,3,2,0:T(8,128)(2,1)S(1)} %bitcast.754, f32[2,6,784,196]{2,3,1,0:T(8,128)} %fusion.356, f32[2,6,784]{2,1,0:T(8,128)S(1)} %get-tuple-element.1137, f32[2,6,784]{2,1,0:T(8,128)S(1)} %get-tuple-element.1138, pred[2,784,196]{1,2,0:T(8,128)(4,1)S(1)} %broadcast_compare_fusion.8, ...), kind=kOutput, calls=%fused_computation.48.clone.1 | convolution fusion | flops 483571200 | bytes 11672193 | tf_op jit(solution)/shard_map/while/body/eval_jaxpr/shqk,sqhd->skhd/dot_general | solution.py:279
  493.9 7.0 fusion.358
  509.4 4.9 fusion.356
  515.6 4.8 copy.475
  520.5 9.1 %fusion.357 = f32[2,196,6,64]{1,3,2,0:T(8,128)} fusion(bf16[2,784,6,64]{1,3,2,0:T(8,128)(2,1)S(1)} %bitcast.754, f32[2,6,784,196]{2,3,1,0:T(8,128)} %fusion.356, f32[2,6,784]{2,1,0:T(8,128)S(1)} %get-tuple-element.1137, f32[2,6,784]{2,1,0:T(8,128)S(1)} %get-tuple-element.1138, pred[2,784,196]{1,2,0:T(8,128)(4,1)S(1)} %broadcast_compare_fusion.8, ...), kind=kOutput, calls=%fused_computation.48.clone.1 | convolution fusion | flops 483571200 | bytes 11672193 | tf_op jit(solution)/shard_map/while/body/eval_jaxpr/shqk,sqhd->skhd/dot_general | solution.py:279
  529.6 7.1 fusion.358
  545.2 4.9 fusion.356
  551.4 4.8 copy.475
  556.3 9.1 %fusion.357 = f32[2,196,6,64]{1,3,2,0:T(8,128)} fusion(bf16[2,784,6,64]{1,3,2,0:T(8,128)(2,1)S(1)} %bitcast.754, f32[2,6,784,196]{2,3,1,0:T(8,128)} %fusion.356, f32[2,6,784]{2,1,0:T(8,128)S(1)} %get-tuple-element.1137, f32[2,6,784]{2,1,0:T(8,128)S(1)} %get-tuple-element.1138, pred[2,784,196]{1,2,0:T(8,128)(4,1)S(1)} %broadcast_compare_fusion.8, ...), kind=kOutput, calls=%fused_computation.48.clone.1 | convolution fusion | flops 483571200 | bytes 11672193 | tf_op jit(solution)/shard_map/while/body/eval_jaxpr/shqk,sqhd->skhd/dot_general | solution.py:279
  565.4 7.1 fusion.358
  581.0 4.9 fusion.356
  592.0 9.1 %fusion.357 = f32[2,196,6,64]{1,3,2,0:T(8,128)} fusion(bf16[2,784,6,64]{1,3,2,0:T(8,128)(2,1)S(1)} %bitcast.754, f32[2,6,784,196]{2,3,1,0:T(8,128)} %fusion.356, f32[2,6,784]{2,1,0:T(8,128)S(1)} %get-tuple-element.1137, f32[2,6,784]{2,1,0:T(8,128)S(1)} %get-tuple-element.1138, pred[2,784,196]{1,2,0:T(8,128)(4,1)S(1)} %broadcast_compare_fusion.8, ...), kind=kOutput, calls=%fused_computation.48.clone.1 | convolution fusion | flops 483571200 | bytes 11672193 | tf_op jit(solution)/shard_map/while/body/eval_jaxpr/shqk,sqhd->skhd/dot_general | solution.py:279
  601.2 7.1 fusion.358
  618.5 8.2 pad_maximum_fusion
  626.8 164.4 %all-reduce.75.cloned.1.call-done = (f32[1769472]{0:T(1024)}, f32[8,3,3,384]{3,0,2,1:T(8,128)}) async-done(((f32[1769472]{0:T(1024)}, f32[8,3,3,384]{3,0,2,1:T(8,128)}), (f32[1769472]{0:T(1024)}, f32[8,3,3,384]{3,0,2,1:T(8,128)})) %all-reduce.75.cloned.1.call-update) | async-done | bytes 7188496
  808.3 42.3 %all-reduce.71 = (f32[384]{0:T(512)}, f32[384]{0:T(512)}, f32[384]{0:T(512)}, f32[3,8,3,3,8]{4,1,3,2,0:T(8,128)}) all-reduce(f32[384]{0:T(512)S(1)} %get-tuple-element.825, f32[384]{0:T(512)S(1)} %copy-done.92, f32[384]{0:T(512)S(1)} %copy-done.91, ...), channel_id=1, replica_groups=mesh['frame'=16,'seq'=2] {'frame','seq'}, use_global_device_ids=true, to_apply=%region_22.23 | all-reduce | flops 2880 | bytes 23040 | tf_op jit(solution)/shard_map/psum | solution.py:315
  850.6 17.8 %all-gather.15.cloned.1.call-done = f32[1769472]{0:T(1024)} async-done(((f32[55296]{0:T(1024)}), f32[1769472]{0:T(1024)}) %all-gather.15.cloned.1.call-update) | async-done | bytes 7077904 | tf_op jit(solution)/shard_map/all_gather | solution.py:319
  (494 shorter events, 230.5 us)
Async XLA Ops:
  7.2 224.7 %copy-start = (bf16[384,1536]{1,0:T(8,128)(2,1)S(1)}, bf16[384,1536]{1,0:T(8,128)(2,1)}, u32[]{:S(2)}) copy-start(bf16[384,1536]{1,0:T(8,128)(2,1)} %param.24) | copy-start | bytes 3538948
  7.2 6.1 copy-start.89
  7.2 66.0 %all-gather.7.cloned.1.call-start = ((), (), s32[]{:S(2)}) async-start(), calls=%async_computation | async-start | bytes 5117952 | tf_op jit(solution)/shard_map/all_gather | solution.py:171
  11.4 218.7 %copy-start.17 = (f32[392,384]{1,0:T(8,128)}, f32[392,384]{1,0:T(8,128)S(1)}, u32[]{:S(2)}) copy-start(f32[392,384]{1,0:T(8,128)S(1)} %reshape.302) | copy-start | bytes 1806340
  16.4 112.1 %all-gather.9.cloned.1.call-start = ((), (), s32[]{:S(2)}) async-start(), calls=%async_computation.1 | async-start | bytes 5117952 | tf_op jit(solution)/shard_map/all_gather | solution.py:172
  17.5 447.7 %all-gather.11.cloned.1.call-start = ((), (), s32[]{:S(2)}) async-start(), calls=%async_computation.2 | async-start | bytes 5117952 | tf_op jit(solution)/shard_map/all_gather | solution.py:297
  17.5 5.1 copy-start.56
  18.6 29.4 %copy-start.75 = (bf16[3,8,3,3,8]{4,1,3,2,0:T(8,128)(2,1)S(1)}, bf16[3,8,3,3,8]{4,1,3,2,0:T(8,128)(2,1)}, u32[]{:S(2)}) copy-start(bf16[3,8,3,3,8]{4,1,3,2,0:T(8,128)(2,1)} %param.28) | copy-start | bytes 10372
  18.6 446.6 %all-gather.13.cloned.1.call-start = ((), (), s32[]{:S(2)}) async-start(), calls=%async_computation.3 | async-start | bytes 5117952 | tf_op jit(solution)/shard_map/all_gather | solution.py:298
  48.7 194.0 %copy-start.62 = (bf16[8,3,3,8]{3,0,2,1:T(8,128)(2,1)}, bf16[8,3,3,8]{3,0,2,1:T(8,128)(2,1)S(1)}, u32[]{:S(2)}) copy-start(bf16[8,3,3,8]{3,0,2,1:T(8,128)(2,1)S(1)} %get-tuple-element.919) | copy-start | bytes 3460
  152.5 6.6 copy-start.2
  173.7 6.1 copy-start.2
  194.6 6.0 copy-start.2
  215.3 6.0 copy-start.2
  227.0 4.8 copy-start.78
  234.9 4.6 copy-start.60
  236.1 26.2 %copy-start.9 = (f32[2,14,14,384]{3,2,1,0:T(8,128)}, f32[2,14,14,384]{3,2,1,0:T(8,128)S(1)}, u32[]{:S(2)}) copy-start(f32[2,14,14,384]{3,2,1,0:T(8,128)S(1)} %reshape.305) | copy-start | bytes 1806340
  240.7 19.0 %copy-start.43 = (f32[2,14,14,8,1]{2,3,4,1,0:T(8,128)}, f32[2,14,14,8,1]{2,3,4,1,0:T(8,128)S(1)}, u32[]{:S(2)}) copy-start(f32[2,14,14,8,1]{2,3,4,1,0:T(8,128)S(1)} %get-tuple-element.900) | copy-start | bytes 37636
  243.0 14.0 %copy-start.45 = (f32[2,14,14,8]{2,3,1,0:T(8,128)}, f32[2,14,14,8]{2,3,1,0:T(8,128)S(1)}, u32[]{:S(2)}) copy-start(f32[2,14,14,8]{2,3,1,0:T(8,128)S(1)} %get-tuple-element.926) | copy-start | bytes 37636
  245.3 6.6 copy-start.15
  245.3 8.0 copy-start.47
  247.6 14.7 %copy-start.33 = (f32[2,14,14,8]{2,3,1,0:T(8,128)}, f32[2,14,14,8]{2,3,1,0:T(8,128)S(1)}, u32[]{:S(2)}) copy-start(f32[2,14,14,8]{2,3,1,0:T(8,128)S(1)} %fusion.62) | copy-start | bytes 37636
  247.6 6.5 copy-start.51
  253.5 4.9 copy-start.3
  263.3 6.5 copy-start.26
  270.3 191.2 %copy-start.20 = (f32[392,384]{1,0:T(8,128)}, f32[392,384]{1,0:T(8,128)S(1)}, u32[]{:S(2)}) copy-start(f32[392,384]{1,0:T(8,128)S(1)} %add_add_fusion.4) | copy-start | bytes 1806340
  275.7 515.6 %all-reduce.75.cloned.1.call-start = ((), (), s32[]{:S(2)}) async-start(), calls=%async_computation.5 | async-start | bytes 14376960
  395.8 4.7 copy-start.52
  442.4 4.7 copy-start.27
  478.7 6.2 copy-start.59
  514.3 6.2 copy-start.59
  550.1 6.2 copy-start.59
  585.8 6.2 copy-start.59
  613.9 4.6 copy-start.29
  626.7 166.2 %copy-start.6 = (f32[2,14,14,8]{2,3,1,0:T(8,128)S(1)}, f32[2,14,14,8]{2,3,1,0:T(8,128)}, u32[]{:S(2)}) copy-start(f32[2,14,14,8]{2,3,1,0:T(8,128)} %copy-done.5) | copy-start | bytes 37636
  626.7 166.2 %copy-start.16 = (f32[2,14,14,8]{2,3,1,0:T(8,128)S(1)}, f32[2,14,14,8]{2,3,1,0:T(8,128)}, u32[]{:S(2)}) copy-start(f32[2,14,14,8]{2,3,1,0:T(8,128)} %copy-done.15) | copy-start | bytes 37636
  626.7 169.4 %copy-start.48 = (f32[2,14,14,8]{2,3,1,0:T(8,128)S(1)}, f32[2,14,14,8]{2,3,1,0:T(8,128)}, u32[]{:S(2)}) copy-start(f32[2,14,14,8]{2,3,1,0:T(8,128)} %copy-done.47) | copy-start | bytes 37636
  626.7 169.9 %copy-start.8 = (f32[2,14,14,8]{2,3,1,0:T(8,128)S(1)}, f32[2,14,14,8]{2,3,1,0:T(8,128)}, u32[]{:S(2)}) copy-start(f32[2,14,14,8]{2,3,1,0:T(8,128)} %copy-done.7) | copy-start | bytes 37636
  626.8 169.9 %copy-start.12 = (f32[2,14,14,8]{2,3,1,0:T(8,128)S(1)}, f32[2,14,14,8]{2,3,1,0:T(8,128)}, u32[]{:S(2)}) copy-start(f32[2,14,14,8]{2,3,1,0:T(8,128)} %copy-done.11) | copy-start | bytes 37636
  626.8 241.7 %all-gather.15.cloned.1.call-start = ((), (), s32[]{:S(2)}) async-start(), calls=%async_computation.4 | async-start | bytes 7299072 | tf_op jit(solution)/shard_map/all_gather | solution.py:319
  626.8 173.1 %copy-start.4 = (f32[2,14,14,8]{2,3,1,0:T(8,128)S(1)}, f32[2,14,14,8]{2,3,1,0:T(8,128)}, u32[]{:S(2)}) copy-start(f32[2,14,14,8]{2,3,1,0:T(8,128)} %copy-done.3) | copy-start | bytes 37636
  626.8 173.1 %copy-start.14 = (f32[2,14,14,8]{2,3,1,0:T(8,128)S(1)}, f32[2,14,14,8]{2,3,1,0:T(8,128)}, u32[]{:S(2)}) copy-start(f32[2,14,14,8]{2,3,1,0:T(8,128)} %copy-done.13) | copy-start | bytes 37636
  795.0 8.2 copy-start.44
  795.4 8.1 copy-start.46
  796.5 7.4 copy-start.10
  796.5 7.4 copy-start.34
  797.8 7.8 copy-start.30
  797.8 7.8 copy-start.49
  (60 other events, 154.7 us)
Sparse Core Ops, SparseCore 0:
  16.5 56.6 all-gather.6
  76.0 52.4 all-gather.8
  130.7 52.4 all-gather.10
  275.8 52.3 all-gather.12
  626.9 164.3 all-reduce.74
  795.0 73.4 all-gather.14
where the time goes:
time: 897 us; the launch traced here: 890 us
  waiting for transfers between devices  244 us (27%)
  matrix products  238 us (27%)
  local copies, waits for them, and re-layouts  192 us (21%)
  blocking collectives  150 us (17%)
  other arithmetic  49.6 us (6%)
  between operations  16.2 us (2%)
    unnamed x7, waiting for transfers between devices  165 us
    dynamic_slice x20, local copies, waits for them, and re-layouts, one_block(): lax.dynamic_slice_in_dim(piece, offset, block_len, 1)  87.9 us
    unnamed x210, local copies, waits for them, and re-layouts  55.8 us
    all_gather x1, blocking collectives, on_device(): lax.all_gather(log_total, 'frame', axis=2, tiled=True)  42.3 us
    psum x1, blocking collectives, on_device(): lax.psum((d_g_attn, d_g_mlp, d_g_learn, d_conv_first, d_rest), ('frame',...  42.3 us
    all_gather x1, blocking collectives, on_device(): lax.all_gather(delta_row, 'frame', axis=2, tiled=True)  42 us
    all_gather x1, waiting for transfers between devices, on_device(): lax.all_gather(value_rows, 'frame', axis=1, tiled=True)  41.1 us
    dot_general x4, matrix products, query_grad_block(): jnp.einsum('shqk,skhd->sqhd', d_scores, key_heads, preferred_element_type...  37.1 us
  transfers between devices with their start and end apart: 6, of which 4 were waited for; matrix products, arithmetic and copies ran while one was open for 32% of the time, Pallas kernels for 0%

commit v1 on v0

v1 whole, which is shorter than its diff:
```python
import functools

import jax
import jax.numpy as jnp
import numpy as np
from jax import lax
from jax.experimental import pallas as pl
from jax.experimental.pallas import tpu as pltpu
from jax.sharding import PartitionSpec as P

HEADS = 6
HEAD_DIM = 64
MAPS = 8
GRID = 14
CELLS = GRID * GRID
PAIRS = HEADS // 2
WIDE = 512
BIG = 1e30
LSE0 = 4
DEL0 = 4 + 3 * HEADS
AUG_END = 4 + 6 * HEADS
F32 = jnp.float32
BF16 = jnp.bfloat16
HIGH = lax.Precision.HIGHEST
MESH = pl.DeviceIdType.MESH
VMEM = pltpu.VMEM
MIB = 1 << 20


def nn(a, b, precision=None):
    return lax.dot_general(a, b, (((1,), (0,)), ((), ())), precision=precision, preferred_element_type=F32)


def nt(a, b, precision=None):
    return lax.dot_general(a, b, (((1,), (1,)), ((), ())), precision=precision, preferred_element_type=F32)


def tn(a, b, precision=None):
    return lax.dot_general(a, b, (((0,), (0,)), ((), ())), precision=precision, preferred_element_type=F32)


def iota(shape, dim):
    return lax.broadcasted_iota(jnp.int32, shape, dim)


def sixteen(v):
    return jnp.concatenate([v, jnp.zeros((8, v.shape[1]), v.dtype)], axis=0)


def normed(x):
    centered = x - jnp.mean(x, axis=-1, keepdims=True)
    rstd = lax.rsqrt(jnp.mean(centered * centered, axis=-1, keepdims=True) + 1e-06)
    return centered * rstd, rstd


def norm_back(vhat, rstd, dout, gain):
    e = dout * gain
    mean_e = jnp.mean(e, axis=-1, keepdims=True)
    mean_ev = jnp.mean(e * vhat, axis=-1, keepdims=True)
    return rstd * (e - mean_e - vhat * mean_ev), jnp.sum(dout * vhat, axis=0, keepdims=True)


C0 = 0.7978845608028654
C1 = 0.044715


def gelu(u):
    return 0.5 * u * (1.0 + jnp.tanh(C0 * (u + C1 * u * u * u)))


def gelu_grad(u):
    t = jnp.tanh(C0 * (u + C1 * u * u * u))
    return 0.5 * (1.0 + t) + 0.5 * u * (1.0 - t * t) * (C0 + (3.0 * C0 * C1) * u * u)


def flip(v, b):
    return v + b * (1 - 2 * ((v // b) % 2))


def bit_of(v, b):
    return (v // b) % 2


def rc(src, dst, send, recv, dev):
    return pltpu.make_async_remote_copy(
        src_ref=src, dst_ref=dst, send_sem=send, recv_sem=recv, device_id=dev, device_id_type=MESH
    )


def greet(partners):
    barrier = pltpu.get_barrier_semaphore()
    for dev in partners:
        pl.semaphore_signal(barrier, inc=1, device_id=dev, device_id_type=MESH)
    pl.semaphore_wait(barrier, len(partners))


def gather_half(half, own_slots, slot_ref, send, recv, fi, si, counter):
    g = fi % half
    other_bits = []
    b = 2
    while b < half:
        other_bits.append(b)
        b *= 2
    n = len(other_bits)
    parts = []
    for k, (base, ready) in enumerate(own_slots):
        order = other_bits[k % n :] + other_bits[: k % n] if n else []
        parts.append((base, ready, order))
    sends = []

    def push(slot, bit):
        k = counter[0]
        counter[0] += 1
        ref = slot_ref(slot)
        cp = rc(ref, ref, send.at[k], recv.at[slot], (flip(fi, bit), si))
        cp.start()
        sends.append(cp)

    def wait_slot(slot):
        ref = slot_ref(slot)
        rc(ref, ref, send.at[0], recv.at[slot], (flip(fi, 1), si)).wait_recv()

    arrived = []
    for base, ready, order in parts:
        if ready is not None:
            ready()
        for bit in order:
            push(base + g, bit)
        push(base + g, 1)
    for step in range(n):
        for base, _, order in parts:
            have = [g]
            for bit in order[:step]:
                have = have + [flip(h, bit) for h in have]
            new = [flip(h, order[step]) for h in have]
            for slot in new:
                wait_slot(base + slot)
                for bit in order[step + 1 :]:
                    push(base + slot, bit)
                push(base + slot, 1)
    for base, _, order in parts:
        have = [g]
        for bit in order:
            have = have + [flip(h, bit) for h in have]
        for h in have:
            wait_slot(base + flip(h, 1))
    for cp in sends:
        cp.wait_send()


def half_partners(half, fi, si):
    out = []
    b = 1
    while b < half:
        out.append((flip(fi, b), si))
        b *= 2
    return out


def token_gather_kernel(frames, cells, tokens, segments, d_learned, xg_ref, xp_ref, slots, send, recv):
    half = frames // 2
    fi = lax.axis_index("frame")
    si = lax.axis_index("seq")
    mine = fi // half
    partner = (fi + half * (1 - 2 * mine), si)
    rows, width = xp_ref.shape[1:]
    for k in range(2):
        body = tokens[k].astype(F32)[0:cells]
        seg = jnp.broadcast_to(segments[k : k + 1, 0:1].astype(F32), (1, width))
        dl = d_learned[k]
        pad = jnp.zeros((rows - body.shape[0] - 1 - MAPS, width), F32)
        xp_ref[k] = jnp.concatenate([body, seg, dl, pad], axis=0).astype(BF16)
    greet(half_partners(half, fi, si) + [partner])
    counter = [1]
    cp = rc(xp_ref.at[1 - mine], slots.at[fi], send.at[0], recv.at[fi], partner)
    cp.start()
    slots[fi] = xp_ref[mine]

    def partner_here():
        slot = fi + half * (1 - 2 * mine)
        rc(slots.at[slot], slots.at[slot], send.at[0], recv.at[slot], partner).wait_recv()

    gather_half(
        half,
        [(half * mine, None), (half * (1 - mine), partner_here)],
        lambda s: slots.at[s],
        send,
        recv,
        fi,
        si,
        counter,
    )
    cp.wait_send()
    xg_ref[...] = slots[...]


def da_gather_kernel(frames, rows, da_ref, dag_ref, slots, send, recv):
    half = frames // 2
    fi = lax.axis_index("frame")
    si = lax.axis_index("seq")
    greet(half_partners(half, fi, si))
    g = fi % half
    slots[:, pl.ds(pl.multiple_of(g * rows, rows), rows), :] = da_ref[:, :rows, :]
    slots[:, pl.ds(pl.multiple_of((g + half) * rows, rows), rows), :] = da_ref[:, rows:, :]
    gather_half(
        half,
        [(0, None), (half, None)],
        lambda s: slots.at[:, pl.ds(pl.multiple_of(s * rows, rows), rows), :],
        send,
        recv,
        fi,
        si,
        [0],
    )
    dag_ref[...] = slots[...]


def aug_masks(h):
    lane = iota((1, 128), 1)
    seg = lane < 4
    lse = seg | ((lane >= LSE0 + 3 * h) & (lane < LSE0 + 3 * h + 3))
    dlt = (lane >= DEL0 + 3 * h) & (lane < DEL0 + 3 * h + 3)
    return lse.astype(F32).astype(BF16), dlt.astype(F32).astype(BF16)


def pieces(value, which):
    hi = value.astype(BF16).astype(F32)
    rest = value - hi
    mid = rest.astype(BF16).astype(F32)
    low = rest - mid
    return jnp.where(which == 0, hi, jnp.where(which == 1, mid, low))


def half_masks():
    lane = iota((1, 128), 1)
    first = (lane < HEAD_DIM).astype(F32).astype(BF16)
    return first, (lane >= HEAD_DIM).astype(F32).astype(BF16)


def layer_kernel(
    frames,
    rows,
    cells,
    xg,
    g_attn,
    w_qkv,
    w_out,
    g_mlp,
    w_up,
    w_down,
    g_learn,
    first9,
    rest27,
    tapmask,
    blockones,
    qkv,
    augk,
    da_ext,
    dx2_ref,
    learned,
    grads,
    augq,
    o_scr,
    x2_scr,
    y_scr,
    vhat2_scr,
    vhat3_scr,
    rstd2_scr,
    rstd3_scr,
    dh2_scr,
    u_scr,
    hid_scr,
    h2_scr,
    a_scr,
    dm_scr,
    h3p,
    yp,
    dyp,
    w72_scr,
    spread_scr,
    rest_scr,
    gain_scr,
    conv_bw,
    conv_fw,
):
    fi = lax.axis_index("frame")
    half = frames // 2
    g = fi % half
    own = 2 * rows
    lane128 = iota((rows, 128), 1)
    row128 = iota((rows, 128), 0)
    valid_row = row128 < cells

    w72 = first9[...].reshape(72, 384)
    w72_scr[...] = sixteen(w72).astype(BF16)
    square_r, square_c = iota((128, 128), 0), iota((128, 128), 1)
    repeat = ((square_c & 7) == square_r).astype(F32)
    same_tap = (((square_r >> 3) == (square_c >> 3)) & (square_r < 72)).astype(F32)
    for layer in range(3):
        by_tap = rest27[9 * layer : 9 * layer + 9].reshape(72, MAPS)
        by_tap = jnp.concatenate([by_tap, jnp.zeros((72, 120), F32)], axis=1)
        conv_bw[layer] = sixteen(by_tap)
        by_tap = jnp.concatenate([by_tap, jnp.zeros((56, 128), F32)], axis=0)
        conv_fw[layer] = nn(repeat[0:16], nn(by_tap, repeat, HIGH) * same_tap, HIGH)

    def project(f, carry):
        x = xg[f].astype(F32)
        seg = x[cells : cells + 1, 0:128]
        x = jnp.where(iota(x.shape, 0) < cells, x, 0.0)
        vhat, _ = normed(x)
        h1 = (vhat * g_attn[...].reshape(1, -1)).astype(BF16)
        base = pl.multiple_of(f * rows, rows)
        whole = nn(h1, w_qkv[...])
        for b in range(9):
            part = whole[:, 128 * b : 128 * b + 128]
            if b < 3:
                part = part * HEAD_DIM**-0.5
            qkv[b, pl.ds(base, rows), :] = part.astype(BF16)
        same = (lane128.astype(F32) == seg) & valid_row
        augk[pl.ds(base, rows), :] = jnp.where(
            lane128 < 4, jnp.where(same, 0.0, -BIG), jnp.where(lane128 < AUG_END, -1.0, 0.0)
        ).astype(BF16)
        return carry

    lax.fori_loop(0, frames, project, 0)

    first, second = half_masks()
    ones = jnp.ones((frames * rows, 128), BF16)

    for k in range(2):
        f = g + half * k
        seg = xg[f].astype(F32)[cells : cells + 1, 0:128]
        same = (lane128.astype(F32) == seg) & valid_row & (lane128 < 4)
        augq[k * rows : (k + 1) * rows, :] = same.astype(F32)

    def attend(step, carry):
        p = step // 2
        k = step % 2
        f = g + half * k
        q = qkv[p, pl.ds(pl.multiple_of(f * rows, rows), rows), :]
        mine = pl.ds(pl.multiple_of(k * rows, rows), rows)
        aug = augq[mine, :]
        seg_aug = jnp.where(lane128 < 4, aug, 0.0).astype(BF16)
        keys = jnp.concatenate([qkv[3 + p], augk[...]], axis=1)
        values = jnp.concatenate([qkv[6 + p], ones], axis=1)
        outs = []
        for e, keep in enumerate((first, second)):
            s = nt(jnp.concatenate([q * keep, seg_aug], axis=1), keys)
            top = jnp.max(s, axis=1, keepdims=True)
            prob = jnp.exp(s - top).astype(BF16)
            o = nn(prob, values)
            total = o[:, 128:]
            outs.append(o[:, :128] / total)
            lse = top + jnp.log(total)
            lane0 = LSE0 + 3 * (2 * p + e)
            which = lane128 - lane0
            aug = jnp.where((which >= 0) & (which < 3), pieces(lse, which), aug)
        augq[mine, :] = aug
        o_scr[p, mine, :] = jnp.where(lane128 < HEAD_DIM, outs[0], outs[1])
        return carry

    lax.fori_loop(0, 2 * PAIRS, attend, 0)

    def apart(fn):
        pl.when(fi >= 0)(fn)

    @apart
    def _():
        a = jnp.concatenate([o_scr[p].astype(BF16) for p in range(PAIRS)], axis=1)
        a_scr[...] = a
        both = jnp.concatenate([xg[g], xg[g + half]], axis=0).astype(F32)
        r = iota(both.shape, 0)
        x = jnp.where((r < cells) | ((r >= rows) & (r < rows + cells)), both, 0.0)
        x2 = x + nn(a, w_out[...])
        x2_scr[...] = x2
        y_scr[...] = x2
        vhat, rstd = normed(x2)
        rstd2_scr[...] = jnp.broadcast_to(rstd, (own, 128))
        vhat2_scr[...] = vhat
        h2_scr[...] = (vhat * g_mlp[...].reshape(1, -1)).astype(BF16)

    def mlp(j, carry):
        cols = pl.ds(pl.multiple_of(384 * j, 384), 384)
        u = nn(h2_scr[...], w_up[:, cols])
        u_scr[j] = u
        hid = gelu(u).astype(BF16)
        hid_scr[j] = hid
        y_scr[...] += nn(hid, w_down[cols, :])
        return carry

    lax.fori_loop(0, 4, mlp, 0)

    @apart
    def _():
        y = y_scr[...]
        vhat, rstd = normed(y)
        vhat3_scr[...] = vhat
        rstd3_scr[...] = jnp.broadcast_to(rstd, (own, 128))
        h3 = (vhat * g_learn[...].reshape(1, -1)).astype(BF16)
        for k in range(2):
            yp[256 * k : 256 * k + rows, :] = y[k * rows : (k + 1) * rows, :]
            yp[256 * k + rows : 256 * k + 256, :] = jnp.zeros((256 - rows, 384), F32)
            h3p[256 * k : 256 * k + rows, :] = h3[k * rows : (k + 1) * rows, :]
            h3p[256 * k + rows : 256 * k + 256, :] = jnp.zeros((256 - rows, 384), BF16)

    def shift_of(t):
        return GRID * (t // 3 - 1) + (t % 3 - 1)

    def moved(v, s):
        return v if s == 0 else pltpu.roll(v, (-s) % WIDE, 1)

    def tap(t):
        return tapmask[t : t + 1, :]

    def im2col(v):
        parts = [moved(v, shift_of(t)) * tap(t) for t in range(9)]
        return jnp.concatenate(parts + [jnp.zeros((56, WIDE), F32)], axis=0)

    def spread_of(v):
        return jnp.concatenate([moved(v, -shift_of(t)) * tap(8 - t) for t in range(9)], axis=0)

    @apart
    def _():
        taps = nt(w72_scr[...], h3p[...])
        z1 = jnp.zeros((MAPS, WIDE), F32)
        for t in range(9):
            z1 = z1 + moved(taps[8 * t : 8 * t + 8, :], shift_of(t)) * tap(t)
        zs = [z1]
        cols_of = []
        for layer in range(3):
            col = im2col(gelu(zs[-1]))
            cols_of.append(col)
            zs.append(nn(conv_fw[layer], col, HIGH)[0:MAPS])
        maps = tap(4) / (1.0 + jnp.exp(-zs[3]))
        dmaps = []
        for k in range(2):
            f = g + half * k
            dl = xg[f].astype(F32)[cells + 1 : cells + 1 + MAPS, :] * (1.0 / cells)
            dl = sixteen(dl)
            mk = sixteen(maps[:, 256 * k : 256 * k + 256])
            yk = yp[256 * k : 256 * k + 256, :]
            learned[k] = nn(mk, yk, HIGH)[0:MAPS] * (1.0 / cells)
            dmaps.append(nt(dl, yk, HIGH)[0:MAPS])
            dyp[256 * k : 256 * k + 256, :] = tn(mk, dl, HIGH)
        dz = jnp.concatenate(dmaps, axis=1) * maps * (1.0 - maps)
        small = []
        for layer in (2, 1, 0):
            dw = nt(sixteen(dz), cols_of[layer], HIGH)[0:MAPS]
            small.insert(0, jnp.concatenate([dw, jnp.zeros((MAPS, 256), F32)], axis=1))
            dz = tn(conv_bw[layer], sixteen(spread_of(dz)), HIGH)[0:MAPS] * gelu_grad(zs[layer])
        dz = dz.astype(BF16).astype(F32) * tap(4)
        spread_scr[...] = sixteen(spread_of(dz)).astype(BF16)
        rest_scr[...] = jnp.concatenate(small + [jnp.zeros((8, 384), F32)], axis=0)

    @apart
    def _():
        dh3 = tn(spread_scr[...], w72_scr[...])
        dh3 = jnp.concatenate([dh3[0:rows], dh3[256 : 256 + rows]], axis=0)
        dy, dg3 = norm_back(vhat3_scr[...], rstd3_scr[:, 0:1], dh3, g_learn[...].reshape(1, -1))
        dy = dy + jnp.concatenate([dyp[0:rows, :], dyp[256 : 256 + rows, :]], axis=0)
        y_scr[...] = dy
        dm_scr[...] = dy.astype(BF16)
        dh2_scr[...] = jnp.zeros((own, 384), F32)
        gain_scr[...] = jnp.concatenate([dg3, jnp.zeros((7, 384), F32)], axis=0)

    def mlp_back(j, carry):
        cols = pl.ds(pl.multiple_of(384 * j, 384), 384)
        dm = dm_scr[...]
        du = (nt(dm, w_down[cols, :]) * gelu_grad(u_scr[j])).astype(BF16)
        grads[cols, :] = tn(h2_scr[...], du).astype(BF16)
        grads[pl.ds(pl.multiple_of(1536 + 384 * j, 384), 384), :] = tn(hid_scr[j], dm).astype(BF16)
        dh2_scr[...] += nt(du, w_up[:, cols])
        return carry

    lax.fori_loop(0, 4, mlp_back, 0)

    @apart
    def _():
        dx2, dg2 = norm_back(vhat2_scr[...], rstd2_scr[:, 0:1], dh2_scr[...], g_mlp[...].reshape(1, -1))
        dx2 = dx2 + y_scr[...]
        dx2_ref[...] = dx2
        dm_scr[...] = dx2.astype(BF16)
        gains = jnp.concatenate([dg2, gain_scr[0:1, :], jnp.zeros((6, 384), F32)], axis=0)
        d_first = nn(spread_scr[...], h3p[...])[0:72]
        small = [d_first, gains, rest_scr[...], jnp.zeros((16, 384), F32)]
        grads[3456:3584, :] = jnp.concatenate(small, axis=0).astype(BF16)

    @apart
    def _():
        dzz = dm_scr[...]
        grads[3072:3456, :] = tn(a_scr[...], dzz).astype(BF16)
        da = nt(dzz, w_out[...]).astype(BF16)
        prod = jnp.concatenate([o_scr[p] for p in range(PAIRS)], axis=1) * da.astype(F32)
        lane = iota((own, 128), 1)
        which = lane - DEL0
        which = which - 3 * (which // 3)
        delta = pieces(nn(prod, blockones[...], HIGH), which)
        full = jnp.where((lane >= DEL0) & (lane < AUG_END), delta, augq[...])
        for p in range(PAIRS):
            da_ext[p] = da[:, 128 * p : 128 * p + 128]
        da_ext[PAIRS] = full.astype(BF16)


def grad_pass(own_a, own_b, own_aug, all_a, all_b, all_aug, p, total, chunk, with_b):
    rows = own_a.shape[0]
    masks = half_masks()
    left_a, left_b = [], []
    for e in range(2):
        lse_mask, del_mask = aug_masks(2 * p + e)
        left_a.append(jnp.concatenate([own_a * masks[e], own_aug * lse_mask], axis=1))
        left_b.append(jnp.concatenate([own_b * masks[e], own_aug * del_mask], axis=1))

    def body(c, carry):
        here = pl.ds(pl.multiple_of(c * chunk, chunk), chunk)
        ra, rb, aug = all_a(here), all_b(here), all_aug(here)
        right_a = jnp.concatenate([ra, aug], axis=1)
        right_b = jnp.concatenate([rb, aug], axis=1)
        probs = [jnp.exp(nt(left_a[e], right_a)) for e in range(2)]
        ds = [(probs[e] * nt(left_b[e], right_b)).astype(BF16) for e in range(2)]
        new = [carry[0] + nn(jnp.concatenate(ds, axis=1), jnp.concatenate([ra * m for m in masks], axis=0))]
        if with_b:
            both = jnp.concatenate([prob.astype(BF16) for prob in probs], axis=1)
            new.append(carry[1] + nn(both, jnp.concatenate([rb * m for m in masks], axis=0)))
        return tuple(new)

    zero = tuple(jnp.zeros((rows, 128), F32) for _ in range(2 if with_b else 1))
    out = lax.fori_loop(0, total // chunk, body, zero, unroll=True)
    return out if with_b else out[0]


def back_kernel(
    frames, rows, cells, qkv, augk, da_ext, dag, dx2, xg, g_attn, w_qkv, learned, dtok, grads, dqkv
):
    fi = lax.axis_index("frame")
    half = frames // 2
    g = fi % half
    total = frames * rows

    def mine(ref, b):
        at = [ref[b, pl.ds(pl.multiple_of((g + half * k) * rows, rows), rows), :] for k in range(2)]
        return jnp.concatenate(at, axis=0)

    own_augk = jnp.concatenate(
        [augk[pl.ds(pl.multiple_of((g + half * k) * rows, rows), rows), :] for k in range(2)], axis=0
    )

    def query_pass(p, carry):
        dq = grad_pass(
            mine(qkv, p), da_ext[p], da_ext[PAIRS],
            lambda i: qkv[3 + p, i, :], lambda i: qkv[6 + p, i, :], lambda i: augk[i, :],
            p, total, 256, False,
        )
        dqkv[p] = (dq * HEAD_DIM**-0.5).astype(BF16)
        return carry

    lax.fori_loop(0, PAIRS, query_pass, 0)

    def key_pass(p, carry):
        dk, dv = grad_pass(
            mine(qkv, 3 + p), mine(qkv, 6 + p), own_augk,
            lambda i: qkv[p, i, :], lambda i: dag[p, i, :], lambda i: dag[PAIRS, i, :],
            p, total, 256, True,
        )
        dqkv[3 + p] = dk.astype(BF16)
        dqkv[6 + p] = dv.astype(BF16)
        return carry

    lax.fori_loop(0, PAIRS, key_pass, 0)

    x = jnp.concatenate([xg[g], xg[g + half]], axis=0).astype(F32)
    r = iota(x.shape, 0)
    x = jnp.where((r < cells) | ((r >= rows) & (r < rows + cells)), x, 0.0)
    vhat, rstd = normed(x)
    h1 = (vhat * g_attn[...].reshape(1, -1)).astype(BF16)
    dh1 = jnp.zeros(x.shape, F32)
    for b in range(3):
        d = jnp.concatenate([dqkv[3 * b + p] for p in range(PAIRS)], axis=1)
        dh1 = dh1 + nt(d, w_qkv[:, 384 * b : 384 * b + 384])
        grads[384 * b : 384 * b + 384, :] = tn(h1, d).astype(BF16)
    dx, dg = norm_back(vhat, rstd, dh1, g_attn[...].reshape(1, -1))
    grads[1152:1168, :] = jnp.concatenate([dg, jnp.zeros((15, 384), F32)], axis=0).astype(BF16)
    grads[1168:1536, :] = jnp.zeros((368, 384), BF16)
    dx = dx + dx2[...]
    for k in range(2):
        dtok[k, 0:cells, :] = dx[k * rows : k * rows + cells, :]
        tail = jnp.concatenate([learned[k], jnp.zeros((rows - cells - MAPS, 384), F32)], axis=0)
        dtok[k, cells:rows, :] = tail


def mesh_bits(frames, seqs):
    rest = []
    b = 1
    while b < seqs:
        rest.append(("seq", b))
        b *= 2
    b = 2
    while b < frames:
        rest.append(("frame", b))
        b *= 2
    return rest


def neighbour(axis, bit, fi, si):
    return (flip(fi, bit), si) if axis == "frame" else (fi, flip(si, bit))


def coord(axis, bit, fi, si):
    return bit_of(fi, bit) if axis == "frame" else bit_of(si, bit)


CH = 16


def sum_kernel(frames, seqs, rows, cells, early, late, dtok, early_out, late_out, dtok_out, learned_out, buf, land, out, tok_send, tok_land, send, recv, tsem):
    fi = lax.axis_index("frame")
    si = lax.axis_index("seq")
    half = frames // 2
    mine = fi // half
    partner = (fi + half * (1 - 2 * mine), si)
    rest = mesh_bits(frames, seqs)
    everyone = [("frame", 1)] + rest
    greet([neighbour(a, b, fi, si) for a, b in everyone])
    tok_send[...] = dtok[1 - mine].astype(BF16)
    tok_copy = rc(tok_send, tok_land, tsem.at[0], tsem.at[1], partner)
    tok_copy.start()
    n_early = early.shape[0]
    buf[0:n_early, :] = early[...]
    buf[n_early:, :] = late[...]
    third = 1536
    plan = []
    starts = [(0, third), (third, third), (2 * third, 512), (n_early, 1536)]
    for k, (start, length) in enumerate(starts):
        r = k % len(rest)
        plan.append((start, length, [("frame", 1)] + rest[r:] + rest[:r]))
    steps = len(everyone)
    halvings = min(5, steps)
    state = []
    at = 0
    for start, length, order in plan:
        state.append({"seg": start, "len": length, "land": at, "order": order, "hist": []})
        at += length + (steps - halvings) * (length >> halvings)
    sem = [0]

    def next_sem():
        sem[0] += 1
        return sem[0] - 1

    def ds(start, n):
        return pl.ds(pl.multiple_of(start, CH), n)

    for step in range(steps):
        flying = []
        for st in state:
            axis, bit = st["order"][step]
            c = coord(axis, bit, fi, si)
            k = next_sem()
            if step < halvings:
                n = st["len"] // 2
                keep, give = st["seg"] + c * n, st["seg"] + (1 - c) * n
            else:
                n = st["len"]
                keep = give = st["seg"]
            cp = rc(buf.at[ds(give, n), :], land.at[pl.ds(st["land"], n), :], send.at[k], recv.at[k], neighbour(axis, bit, fi, si))
            cp.start()
            flying.append((cp, keep, n))
        for st, (cp, keep, n) in zip(state, flying):
            cp.wait()
            at = st["land"]

            def add(i, carry, keep=keep, at=at):
                there = ds(keep + i * CH, CH)
                buf[there, :] = (buf[there, :].astype(F32) + land[ds(at + i * CH, CH), :].astype(F32)).astype(BF16)
                return carry

            lax.fori_loop(0, n // CH, add, 0)
            st["hist"].append((st["seg"], st["len"]))
            st["seg"], st["len"], st["land"] = keep, n, at + n
    for st in state:
        out[ds(st["seg"], st["len"]), :] = buf[ds(st["seg"], st["len"]), :]
    for step in reversed(range(halvings)):
        flying = []
        for st in state:
            axis, bit = st["order"][step]
            k = next_sem()
            there = out.at[ds(st["seg"], st["len"]), :]
            cp = rc(there, there, send.at[k], recv.at[k], neighbour(axis, bit, fi, si))
            cp.start()
            flying.append(cp)
        for st, cp in zip(state, flying):
            cp.wait()
            st["seg"], st["len"] = st["hist"][step]
    early_out[...] = out[0:n_early, :].astype(F32)
    late_out[...] = out[n_early:, :].astype(F32)
    tok_copy.wait()
    far = tok_land[...].astype(F32)
    dtok_out[mine] = dtok[mine][0:cells, :]
    dtok_out[1 - mine] = far[0:cells, :]
    learned_out[mine] = dtok[mine][cells : cells + MAPS, :]
    learned_out[1 - mine] = far[cells : cells + MAPS, :]


def vspec(n):
    return [pl.BlockSpec(memory_space=VMEM)] * n


def params(collective=None, mib=56):
    if collective is None:
        return pltpu.CompilerParams(vmem_limit_bytes=mib * MIB)
    return pltpu.CompilerParams(collective_id=collective, has_side_effects=True, vmem_limit_bytes=mib * MIB)


def tap_masks():
    p = np.arange(WIDE) % 256
    px, py = p // GRID, p % GRID
    out = np.zeros((16, WIDE), np.float32)
    for t in range(9):
        r, c = t // 3 - 1, t % 3 - 1
        out[t] = (p < CELLS) & (px + r >= 0) & (px + r < GRID) & (py + c >= 0) & (py + c < GRID)
    return out


def head_sums():
    out = np.zeros((HEADS * HEAD_DIM, 128), np.float32)
    for h in range(HEADS):
        out[h * HEAD_DIM : (h + 1) * HEAD_DIM, DEL0 + 3 * h : DEL0 + 3 * h + 3] = 1.0
    return out


def on_device(frames, seqs, tokens, segments, g_attn, w_qkv, w_out, g_mlp, w_up, w_down, g_learn, conv_first, conv_rest, d_learned):
    _, cells, width = tokens.shape
    rows = -(-(cells + 1 + MAPS) // 16) * 16
    own = 2 * rows
    total = frames * rows
    n_sems = 1 + 2 * frames * 4
    sds = jax.ShapeDtypeStruct
    xg = pl.pallas_call(
        functools.partial(token_gather_kernel, frames, cells),
        out_shape=sds((frames, rows, width), BF16),
        in_specs=vspec(3),
        out_specs=vspec(1)[0],
        scratch_shapes=[
            VMEM((2, rows, width), BF16),
            VMEM((frames, rows, width), BF16),
            pltpu.SemaphoreType.DMA((n_sems,)),
            pltpu.SemaphoreType.DMA((frames,)),
        ],
        compiler_params=params(0),
        name="tokens_to_half",
    )(jnp.pad(tokens, ((0, 0), (0, rows - cells), (0, 0))), segments, d_learned.astype(F32))
    first9 = conv_first.transpose(1, 2, 0, 3).reshape(9, MAPS, width).astype(F32)
    rest27 = conv_rest.transpose(0, 2, 3, 1, 4).reshape(27, MAPS, MAPS).astype(F32)
    qkv, augk, da_ext, dx2, learned, early = pl.pallas_call(
        functools.partial(layer_kernel, frames, rows, cells),
        out_shape=[
            sds((9, total, 128), BF16),
            sds((total, 128), BF16),
            sds((PAIRS + 1, own, 128), BF16),
            sds((own, width), F32),
            sds((2, MAPS, width), F32),
            sds((3584, width), BF16),
        ],
        in_specs=vspec(12),
        out_specs=vspec(6),
        scratch_shapes=[
            VMEM((own, 128), F32),
            VMEM((PAIRS, own, 128), F32),
            VMEM((own, width), F32),
            VMEM((own, width), F32),
            VMEM((own, width), F32),
            VMEM((own, width), F32),
            VMEM((own, 128), F32),
            VMEM((own, 128), F32),
            VMEM((own, width), F32),
            VMEM((4, own, width), F32),
            VMEM((4, own, width), BF16),
            VMEM((own, width), BF16),
            VMEM((own, width), BF16),
            VMEM((own, width), BF16),
            VMEM((WIDE, width), BF16),
            VMEM((WIDE, width), F32),
            VMEM((WIDE, width), F32),
            VMEM((80, width), BF16),
            VMEM((80, WIDE), BF16),
            VMEM((32, width), F32),
            VMEM((8, width), F32),
            VMEM((3, 80, 128), F32),
            VMEM((3, 16, 128), F32),
        ],
        compiler_params=params(),
        name="layer",
    )(
        xg, g_attn, w_qkv, w_out, g_mlp, w_up, w_down, g_learn, first9, rest27,
        jnp.asarray(tap_masks()), jnp.asarray(head_sums()),
    )
    dag = pl.pallas_call(
        functools.partial(da_gather_kernel, frames, rows),
        out_shape=sds((PAIRS + 1, total, 128), BF16),
        in_specs=vspec(1),
        out_specs=vspec(1)[0],
        scratch_shapes=[
            VMEM((PAIRS + 1, total, 128), BF16),
            pltpu.SemaphoreType.DMA((n_sems,)),
            pltpu.SemaphoreType.DMA((frames,)),
        ],
        compiler_params=params(1),
        name="grads_to_half",
    )(da_ext)
    dtok, late = pl.pallas_call(
        functools.partial(back_kernel, frames, rows, cells),
        out_shape=[sds((2, rows, width), F32), sds((1536, width), BF16)],
        in_specs=vspec(9),
        out_specs=vspec(2),
        scratch_shapes=[VMEM((9, own, 128), BF16)],
        compiler_params=params(),
        name="attention_back",
    )(qkv, augk, da_ext, dag, dx2, xg, g_attn, w_qkv, learned)
    n_all = 3584 + 1536
    early_sum, late_sum, d_tokens, learned_all = pl.pallas_call(
        functools.partial(sum_kernel, frames, seqs, rows, cells),
        out_shape=[
            sds((3584, width), F32),
            sds((1536, width), F32),
            sds((2, cells, width), F32),
            sds((2, MAPS, width), F32),
        ],
        in_specs=vspec(3),
        out_specs=vspec(4),
        scratch_shapes=[
            VMEM((n_all, width), BF16),
            VMEM((n_all + (n_all >> 5) * max(0, len(mesh_bits(frames, seqs)) - 4), width), BF16),
            VMEM((n_all, width), BF16),
            VMEM((rows, width), BF16),
            VMEM((rows, width), BF16),
            pltpu.SemaphoreType.DMA((64,)),
            pltpu.SemaphoreType.DMA((64,)),
            pltpu.SemaphoreType.DMA((2,)),
        ],
        compiler_params=params(2),
        name="sums",
    )(early, late, dtok)
    d_w_up = jnp.concatenate([early_sum[384 * j : 384 * j + 384] for j in range(4)], axis=1)
    d_w_qkv = jnp.concatenate([late_sum[384 * j : 384 * j + 384] for j in range(3)], axis=1)
    d_first = early_sum[3456 : 3456 + 72].reshape(3, 3, MAPS, width).transpose(2, 0, 1, 3)
    d_rest = early_sum[3536 : 3536 + 24, :72].reshape(3, MAPS, 3, 3, MAPS)
    return (
        learned_all.astype(BF16),
        d_tokens,
        late_sum[1152],
        d_w_qkv,
        early_sum[3072:3456],
        early_sum[3528],
        d_w_up,
        early_sum[1536:3072],
        early_sum[3529],
        d_first,
        d_rest,
    )


def solution(mesh):
    frames, seqs = mesh.shape["frame"], mesh.shape["seq"]
    both = P("seq", "frame", None)
    in_specs = (both, P("seq", "frame"), *([P()] * 9), both)
    out_specs = (both, both, *([P()] * 9))
    return jax.shard_map(
        functools.partial(on_device, frames, seqs),
        mesh=mesh,
        in_specs=in_specs,
        out_specs=out_specs,
        check_vma=False,
    )
```

time: 897 us -> 246 us (0.27)
  waiting for transfers between devices: 244 us -> 0 us
  matrix products: 238 us -> 0 us
  Pallas kernels: 0 us -> 222 us
  local copies, waits for them, and re-layouts: 192 us -> 14.3 us
  blocking collectives: 150 us -> 0 us
  other arithmetic: 49.6 us -> 8.62 us
  between operations: 16.2 us -> 0.69 us
    dot_general x127 -> x0, matrix products: 238 us -> none  [the longest x4 37.1 us: query_grad_block(): jnp.einsum('shqk,skhd->sqhd', d_scores, key_heads, preferred_element_type...]
    pallas_call x0 -> x5, Pallas kernels: none -> 222 us  [the longest x1 77 us: on_device(): pl.pallas_call(functools.partial(sum_kernel, frames, seqs, rows, cells),...]
    unnamed x7 -> x0, waiting for transfers between devices: 165 us -> none
    all_gather x3 -> x0, blocking collectives: 108 us -> none  [the longest x1 42.3 us: on_device(): lax.all_gather(log_total, 'frame', axis=2, tiled=True)]
    dynamic_slice x36 -> x0, local copies, waits for them, and re-layouts: 92.9 us -> none  [the longest x20 87.9 us: one_block(): lax.dynamic_slice_in_dim(piece, offset, block_len, 1)]
    all_gather x5 -> x0, waiting for transfers between devices: 79 us -> none  [the longest x1 41.1 us: on_device(): lax.all_gather(value_rows, 'frame', axis=1, tiled=True)]
    unnamed x210 -> x5, local copies, waits for them, and re-layouts: 55.8 us -> 4.01 us
    psum x1 -> x0, blocking collectives: 42.3 us -> none  [on_device(): lax.psum((d_g_attn, d_g_mlp, d_g_learn, d_conv_first, d_rest), ('frame',...]
  transfers between devices with their start and end apart: 6 -> 0, of which waited for: 4 -> 0; matrix products, arithmetic and copies ran while one was open for 32% -> 0% of each run, Pallas kernels for 0% -> 0%
where the time goes in v1:
time: 246 us
  Pallas kernels  222 us (90%)
  local copies, waits for them, and re-layouts  14.3 us (6%)
  other arithmetic  8.62 us (4%)
    pallas_call x1, Pallas kernels, on_device(): pl.pallas_call(functools.partial(sum_kernel, frames, seqs, rows, cells),...  77 us
    pallas_call x1, Pallas kernels, on_device(): pl.pallas_call(functools.partial(layer_kernel, frames, rows, cells), out_...  51.3 us
    pallas_call x1, Pallas kernels, on_device(): pl.pallas_call(functools.partial(back_kernel, frames, rows, cells), out_s...  41.5 us
    pallas_call x1, Pallas kernels, on_device(): pl.pallas_call(functools.partial(token_gather_kernel, frames, cells), out...  27.1 us
    pallas_call x1, Pallas kernels, on_device(): pl.pallas_call(functools.partial(da_gather_kernel, frames, rows), out_sha...  25.3 us

profile of v1, /device:TPU:0, one launch (start us, length us, event | category | flops | bytes accessed | tf_op | source)
XLA Modules:
  0.0 245.8 jit_solution(2938264452983426386)
XLA Ops:
  0.6 1.3 convert_element_type.22.d_learned
  2.0 1.5 convert_element_type.32
  3.4 1.5 convert_element_type.33
  4.9 1.0 copy.28
  5.9 0.8 pad.4.tokens
  6.7 27.1 %tokens_to_half.1.xg = bf16[16,208,384]{2,1,0:T(8,128)(2,1)} custom-call(bf16[2,208,384]{2,1,0:T(8,128)(2,1)} %pad.4.tokens, s32[2,196]{1,0:T(2,128)} %segments.1, f32[2,8,384]{2,1,0:T(8,128)} %convert_element_type.22.d_learned), custom_call_target="tpu_custom_call" | custom-call | tf_op jit(solution)/shard_map/tokens_to_half/pallas_call | solution.py:736
  33.8 51.3 %layer.1 = (bf16[9,3328,128]{2,1,0:T(8,128)(2,1)}, bf16[3328,128]{1,0:T(8,128)(2,1)}, bf16[4,416,128]{2,1,0:T(8,128)(2,1)}, f32[416,384]{1,0:T(8,128)}, f32[2,8,384]{2,1,0:T(8,128)}, /*index=5*/bf16[3584,384]{1,0:T(8,128)(2,1)}) custom-call(bf16[16,208,384]{2,1,0:T(8,128)(2,1)} %tokens_to_half.1.xg, f32[384]{0:T(512)} %g_attn.3, bf16[384,1152]{1,0:T(8,128)(2,1)} %w_qkv.3, ...), custom_call_target="tpu_custom_call" | custom-call | tf_op jit(solution)/shard_map/layer/pallas_call | solution.py:752
  85.1 25.3 %grads_to_half.1.dag = bf16[4,3328,128]{2,1,0:T(8,128)(2,1)} custom-call(bf16[4,416,128]{2,1,0:T(8,128)(2,1)} %get-tuple-element.26.da_ref.da_ext), custom_call_target="tpu_custom_call" | custom-call | tf_op jit(solution)/shard_map/grads_to_half/pallas_call | solution.py:795
  110.4 41.5 %attention_back.1 = (f32[2,208,384]{2,1,0:T(8,128)}, bf16[1536,384]{1,0:T(8,128)(2,1)}) custom-call(bf16[9,3328,128]{2,1,0:T(8,128)(2,1)} %get-tuple-element.24.qkv, bf16[3328,128]{1,0:T(8,128)(2,1)} %get-tuple-element.25.augk, bf16[4,416,128]{2,1,0:T(8,128)(2,1)} %get-tuple-element.26.da_ref.da_ext, bf16[4,3328,128]{2,1,0:T(8,128)(2,1)} %grads_to_half.1.dag, ...), custom_call_target="tpu_custom_call" | custom-call | tf_op jit(solution)/shard_map/attention_back/pallas_call | solution.py:808
  151.9 77.0 %sums.1 = (f32[3584,384]{1,0:T(8,128)}, f32[1536,384]{1,0:T(8,128)}, f32[2,196,384]{2,1,0:T(8,128)}, f32[2,8,384]{2,1,0:T(8,128)}) custom-call(bf16[3584,384]{1,0:T(8,128)(2,1)} %get-tuple-element.23.early, bf16[1536,384]{1,0:T(8,128)(2,1)} %get-tuple-element.29.late, f32[2,208,384]{2,1,0:T(8,128)} %get-tuple-element.30.dtok), custom_call_target="tpu_custom_call" | custom-call | tf_op jit(solution)/shard_map/sums/pallas_call | solution.py:818
  228.9 1.3 convert_element_type.29
  230.2 1.4 slice_reduce_fusion
  231.6 0.7 slice.55
  232.3 1.5 slice.54
  233.8 0.1 reshape.35
  234.0 0.7 copy.30
  234.6 0.0 copy-start
  234.6 2.4 copy.29
  237.0 3.2 %slice.52 = f32[1536,384]{1,0:T(8,128)} slice(f32[3584,384]{1,0:T(8,128)} %get-tuple-element.34), slice={[1536:3072], [0:384]} | slice | bytes 4718592 | tf_op jit(solution)/shard_map/slice | solution.py:853
  240.2 0.0 copy-done
  240.2 2.6 %fusion = (f32[384,384]{1,0:T(8,128)S(1)}, f32[384,384]{1,0:T(8,128)S(1)}, f32[384,384]{1,0:T(8,128)S(1)}, f32[384,384]{1,0:T(8,128)S(1)}, f32[384,384]{1,0:T(8,...) fusion(f32[3584,384]{1,0:T(8,128)S(1)} %copy-done, f32[1536,384]{1,0:T(8,128)} %get-tuple-element.33), kind=kLoop, calls=%fused_computation.5 | loop fusion | bytes 9437184 | tf_op jit(solution)/shard_map/slice | solution.py:841
  242.8 1.7 pad_maximum_fusion
  244.5 1.3 pad_maximum_fusion.1
Async XLA Ops:
  234.6 5.6 %copy-start = (f32[3584,384]{1,0:T(8,128)S(1)}, f32[3584,384]{1,0:T(8,128)}, u32[]{:S(2)}) copy-start(f32[3584,384]{1,0:T(8,128)} %get-tuple-element.34) | copy-start | bytes 16515076

commit v2 on v1

--- a/solution.py
+++ b/solution.py
@@ -194,25 +194,54 @@
     xg_ref[...] = slots[...]
 
 
-def da_gather_kernel(frames, rows, da_ref, dag_ref, slots, send, recv):
-    half = frames // 2
-    fi = lax.axis_index("frame")
-    si = lax.axis_index("seq")
-    greet(half_partners(half, fi, si))
+def staged_gather(half, bases, slot_ref, send, recv, fi, si):
     g = fi % half
-    slots[:, pl.ds(pl.multiple_of(g * rows, rows), rows), :] = da_ref[:, :rows, :]
-    slots[:, pl.ds(pl.multiple_of((g + half) * rows, rows), rows), :] = da_ref[:, rows:, :]
-    gather_half(
-        half,
-        [(0, None), (half, None)],
-        lambda s: slots.at[:, pl.ds(pl.multiple_of(s * rows, rows), rows), :],
-        send,
-        recv,
-        fi,
-        si,
-        [0],
-    )
-    dag_ref[...] = slots[...]
+    bits = []
+    b = 2
+    while b < half:
+        bits.append(b)
+        b *= 2
+    n = len(bits)
+    count = [0]
+    sends = []
+
+    def plan_push(slot, bit):
+        count[0] += 1
+        return slot, count[0] - 1, (flip(fi, bit), si)
+
+    def copy(slot, k, dev):
+        ref = slot_ref(slot)
+        return rc(ref, ref, send.at[k], recv.at[slot], dev)
+
+    stages = [[] for _ in range(n + 2)]
+    for part, base in enumerate(bases):
+        order = bits[part % n :] + bits[: part % n] if n else []
+        first = [plan_push(base + g, bit) for bit in order] + [plan_push(base + g, 1)]
+        stages[0].append((None, first))
+        have = [g]
+        for step, bit in enumerate(order):
+            new = [flip(h, bit) for h in have]
+            for h in new:
+                follow = [plan_push(base + h, later) for later in order[step + 1 :]] + [plan_push(base + h, 1)]
+                stages[step + 1].append((base + h, follow))
+            have = have + new
+        for h in have:
+            stages[n + 1].append((base + flip(h, 1), []))
+    for stage in stages:
+        for _, pushes in stage:
+            sends.extend(pushes)
+
+    def run(i):
+        for slot, pushes in stages[i]:
+            if slot is not None:
+                copy(slot, 0, (flip(fi, 1), si)).wait_recv()
+            for push in pushes:
+                copy(*push).start()
+        if i == n + 1:
+            for push in sends:
+                copy(*push).wait_send()
+
+    return run, n + 2
 
 
 def aug_masks(h):
@@ -259,6 +288,7 @@
     dx2_ref,
     learned,
     grads,
+    own_x,
     augq,
     o_scr,
     x2_scr,
@@ -368,6 +398,8 @@
     def _():
         a = jnp.concatenate([o_scr[p].astype(BF16) for p in range(PAIRS)], axis=1)
         a_scr[...] = a
+        own_x[0] = xg[g]
+        own_x[1] = xg[g + half]
         both = jnp.concatenate([xg[g], xg[g + half]], axis=0).astype(F32)
         r = iota(both.shape, 0)
         x = jnp.where((r < cells) | ((r >= rows) & (r < rows + cells)), both, 0.0)
@@ -501,90 +533,29 @@
         da_ext[PAIRS] = full.astype(BF16)
 
 
-def grad_pass(own_a, own_b, own_aug, all_a, all_b, all_aug, p, total, chunk, with_b):
-    rows = own_a.shape[0]
+def grad_pass(own_a, own_b, own_aug, all_a, all_b, all_aug, p, count, split, chunk, with_b, at_point):
     masks = half_masks()
     left_a, left_b = [], []
     for e in range(2):
         lse_mask, del_mask = aug_masks(2 * p + e)
         left_a.append(jnp.concatenate([own_a * masks[e], own_aug * lse_mask], axis=1))
         left_b.append(jnp.concatenate([own_b * masks[e], own_aug * del_mask], axis=1))
-
-    def body(c, carry):
-        here = pl.ds(pl.multiple_of(c * chunk, chunk), chunk)
+    acc = [jnp.zeros((own_a.shape[0], 128), F32) for _ in range(2 if with_b else 1)]
+    for c in range(count):
+        here = pl.ds(c * chunk, chunk)
         ra, rb, aug = all_a(here), all_b(here), all_aug(here)
         right_a = jnp.concatenate([ra, aug], axis=1)
         right_b = jnp.concatenate([rb, aug], axis=1)
         probs = [jnp.exp(nt(left_a[e], right_a)) for e in range(2)]
         ds = [(probs[e] * nt(left_b[e], right_b)).astype(BF16) for e in range(2)]
-        new = [carry[0] + nn(jnp.concatenate(ds, axis=1), jnp.concatenate([ra * m for m in masks], axis=0))]
+        acc[0] = acc[0] + nn(jnp.concatenate(ds, axis=1), jnp.concatenate([ra * m for m in masks], axis=0))
         if with_b:
             both = jnp.concatenate([prob.astype(BF16) for prob in probs], axis=1)
-            new.append(carry[1] + nn(both, jnp.concatenate([rb * m for m in masks], axis=0)))
-        return tuple(new)
-
-    zero = tuple(jnp.zeros((rows, 128), F32) for _ in range(2 if with_b else 1))
-    out = lax.fori_loop(0, total // chunk, body, zero, unroll=True)
-    return out if with_b else out[0]
-
-
-def back_kernel(
-    frames, rows, cells, qkv, augk, da_ext, dag, dx2, xg, g_attn, w_qkv, learned, dtok, grads, dqkv
-):
-    fi = lax.axis_index("frame")
-    half = frames // 2
-    g = fi % half
-    total = frames * rows
-
-    def mine(ref, b):
-        at = [ref[b, pl.ds(pl.multiple_of((g + half * k) * rows, rows), rows), :] for k in range(2)]
-        return jnp.concatenate(at, axis=0)
-
-    own_augk = jnp.concatenate(
-        [augk[pl.ds(pl.multiple_of((g + half * k) * rows, rows), rows), :] for k in range(2)], axis=0
-    )
-
-    def query_pass(p, carry):
-        dq = grad_pass(
-            mine(qkv, p), da_ext[p], da_ext[PAIRS],
-            lambda i: qkv[3 + p, i, :], lambda i: qkv[6 + p, i, :], lambda i: augk[i, :],
-            p, total, 256, False,
-        )
-        dqkv[p] = (dq * HEAD_DIM**-0.5).astype(BF16)
-        return carry
-
-    lax.fori_loop(0, PAIRS, query_pass, 0)
-
-    def key_pass(p, carry):
-        dk, dv = grad_pass(
-            mine(qkv, 3 + p), mine(qkv, 6 + p), own_augk,
-            lambda i: qkv[p, i, :], lambda i: dag[p, i, :], lambda i: dag[PAIRS, i, :],
-            p, total, 256, True,
-        )
-        dqkv[3 + p] = dk.astype(BF16)
-        dqkv[6 + p] = dv.astype(BF16)
-        return carry
-
-    lax.fori_loop(0, PAIRS, key_pass, 0)
-
-    x = jnp.concatenate([xg[g], xg[g + half]], axis=0).astype(F32)
-    r = iota(x.shape, 0)
-    x = jnp.where((r < cells) | ((r >= rows) & (r < rows + cells)), x, 0.0)
-    vhat, rstd = normed(x)
-    h1 = (vhat * g_attn[...].reshape(1, -1)).astype(BF16)
-    dh1 = jnp.zeros(x.shape, F32)
-    for b in range(3):
-        d = jnp.concatenate([dqkv[3 * b + p] for p in range(PAIRS)], axis=1)
-        dh1 = dh1 + nt(d, w_qkv[:, 384 * b : 384 * b + 384])
-        grads[384 * b : 384 * b + 384, :] = tn(h1, d).astype(BF16)
-    dx, dg = norm_back(vhat, rstd, dh1, g_attn[...].reshape(1, -1))
-    grads[1152:1168, :] = jnp.concatenate([dg, jnp.zeros((15, 384), F32)], axis=0).astype(BF16)
-    grads[1168:1536, :] = jnp.zeros((368, 384), BF16)
-    dx = dx + dx2[...]
-    for k in range(2):
-        dtok[k, 0:cells, :] = dx[k * rows : k * rows + cells, :]
-        tail = jnp.concatenate([learned[k], jnp.zeros((rows - cells - MAPS, 384), F32)], axis=0)
-        dtok[k, cells:rows, :] = tail
+            acc[1] = acc[1] + nn(both, jnp.concatenate([rb * m for m in masks], axis=0))
+        if c + 1 == split:
+            at_point(0)
+    at_point(1)
+    return acc if with_b else acc[0]
 
 
 def mesh_bits(frames, seqs):
@@ -608,95 +579,269 @@
     return bit_of(fi, bit) if axis == "frame" else bit_of(si, bit)
 
 
-CH = 16
-
-
-def sum_kernel(frames, seqs, rows, cells, early, late, dtok, early_out, late_out, dtok_out, learned_out, buf, land, out, tok_send, tok_land, send, recv, tsem):
+TILE = 16
+
+
+def at_tile(start, n):
+    return pl.ds(start if isinstance(start, int) else pl.multiple_of(start, TILE), n)
+
+
+def landing_rows(length, steps, halvings):
+    return length + max(0, steps - halvings) * (length >> halvings)
+
+
+class Piece:
+    def __init__(self, start, length, order, halvings, land_at, sem_at, fi, si, buf, land, out, send, recv):
+        self.refs = buf, land, out, send, recv
+        self.steps = []
+        seg = start
+        n = length
+        hist = []
+        sem = sem_at
+        for step, (axis, bit) in enumerate(order):
+            dev = neighbour(axis, bit, fi, si)
+            if step < halvings:
+                hist.append((seg, n, dev))
+                c = coord(axis, bit, fi, si)
+                n = n // 2
+                keep, give = seg + c * n, seg + (1 - c) * n
+            else:
+                keep = give = seg
+            self.steps.append(("add", give, keep, n, land_at, dev, sem))
+            seg = keep
+            land_at += n
+            sem += 1
+        self.own = seg, n
+        self.adds = len(order)
+        for old, old_n, dev in reversed(hist):
+            self.steps.append(("copy", seg, seg, n, 0, dev, sem))
+            seg, n = old, old_n
+            sem += 1
+        self.sem_end = sem
+        self.land_end = land_at
+        self.total = len(self.steps)
+
+    def copy(self, i):
+        buf, land, out, send, recv = self.refs
+        kind, give, _, n, at, dev, sem = self.steps[i]
+        if kind == "add":
+            return rc(buf.at[at_tile(give, n), :], land.at[at_tile(at, n), :], send.at[sem], recv.at[sem], dev)
+        there = out.at[at_tile(give, n), :]
+        return rc(there, there, send.at[sem], recv.at[sem], dev)
+
+    def start(self, i):
+        if i < self.total:
+            self.copy(i).start()
+
+    def finish(self, i):
+        if i < 0 or i >= self.total:
+            return
+        buf, land, out, _, _ = self.refs
+        self.copy(i).wait()
+        kind, _, keep, n, at, _, _ = self.steps[i]
+        if kind == "copy":
+            return
+        to = out if i == self.adds - 1 else buf
+        chunk = TILE
+        for k in (2, 3, 4, 6, 8):
+            if n % (TILE * k) == 0:
+                chunk = TILE * k
+
+        def add(j, carry):
+            here = at_tile(keep + j * chunk, chunk)
+            there = at_tile(at + j * chunk, chunk)
+            to[here, :] = (buf[here, :].astype(F32) + land[there, :].astype(F32)).astype(BF16)
+            return carry
+
+        lax.fori_loop(0, n // chunk, add, 0)
+
+
+EARLY = 3584
+LATE = 3 * 384 + 128
+EARLY_CUTS = ((0, 1024), (1024, 1024), (2048, 1536))
+LATE_CUTS = ((EARLY, 384), (EARLY + 384, 384), (EARLY + 768, 512))
+EARLY_HALVINGS = 5
+LATE_HALVINGS = 3
+
+
+def back_kernel(
+    frames, seqs, rows, cells,
+    qkv_hbm, augk_hbm, early_hbm, da_ext, dx2, own_x, g_attn, w_qkv, learned,
+    sums, own_tok, far_tok,
+    qkv, augk, dag, dqkv, h1_scr, dh1_scr, buf, land, out, tok_send, tok_land,
+    fsem, gsend, grecv, psend, precv, tsem,
+):
     fi = lax.axis_index("frame")
     si = lax.axis_index("seq")
     half = frames // 2
+    g = fi % half
     mine = fi // half
-    partner = (fi + half * (1 - 2 * mine), si)
+    total = frames * rows
+    own = 2 * rows
     rest = mesh_bits(frames, seqs)
-    everyone = [("frame", 1)] + rest
-    greet([neighbour(a, b, fi, si) for a, b in everyone])
-    tok_send[...] = dtok[1 - mine].astype(BF16)
-    tok_copy = rc(tok_send, tok_land, tsem.at[0], tsem.at[1], partner)
+    fetch = [
+        pltpu.make_async_copy(early_hbm, buf.at[pl.ds(0, EARLY), :], fsem.at[0]),
+        pltpu.make_async_copy(qkv_hbm, qkv, fsem.at[1]),
+        pltpu.make_async_copy(augk_hbm, augk, fsem.at[2]),
+    ]
+    for cp in fetch:
+        cp.start()
+    for k in range(2):
+        there = pl.ds(pl.multiple_of((g + half * k) * rows, rows), rows)
+        dag[:, there, :] = da_ext[:, k * rows : (k + 1) * rows, :]
+    greet([neighbour(a, b, fi, si) for a, b in [("frame", 1)] + rest])
+    gather, stages = staged_gather(
+        half, [0, half], lambda s: dag.at[:, pl.ds(pl.multiple_of(s * rows, rows), rows), :], gsend, grecv, fi, si
+    )
+    gather(0)
+    refs = fi, si, buf, land, out, psend, precv
+    early, late = [], []
+    land_at = sem_at = 0
+    for group, cuts, halvings in ((early, EARLY_CUTS, EARLY_HALVINGS), (late, LATE_CUTS, LATE_HALVINGS)):
+        for k, (start, length) in enumerate(cuts):
+            r = k % len(rest)
+            order = [("frame", 1)] + rest[r:] + rest[:r]
+            piece = Piece(start, length, order, min(halvings, len(order)), land_at, sem_at, *refs)
+            land_at, sem_at = piece.land_end, piece.sem_end
+            group.append(piece)
+    fetch[0].wait()
+    for piece in early:
+        piece.start(0)
+
+    def early_point(i):
+        for piece in early:
+            piece.finish(i)
+            piece.start(i + 1)
+
+    x = own_x[...].reshape(own, 384).astype(F32)
+    r = iota(x.shape, 0)
+    x = jnp.where((r < cells) | ((r >= rows) & (r < rows + cells)), x, 0.0)
+    vhat, _ = normed(x)
+    h1_scr[...] = (vhat * g_attn[...].reshape(1, -1)).astype(BF16)
+    dh1_scr[...] = jnp.zeros((own, 384), F32)
+    buf[EARLY + 1152 :, :] = jnp.zeros((128, 384), BF16)
+    fetch[1].wait()
+    fetch[2].wait()
+
+    def own_rows(b):
+        at = [qkv[b, pl.ds(pl.multiple_of((g + half * k) * rows, rows), rows), :] for k in range(2)]
+        return jnp.concatenate(at, axis=0)
+
+    own_augk = jnp.concatenate(
+        [augk[pl.ds(pl.multiple_of((g + half * k) * rows, rows), rows), :] for k in range(2)], axis=0
+    )
+    chunk = 256
+    pieces_n = total // chunk
+    split = (pieces_n + 1) // 2
+
+    def query_pass(p, carry):
+        def at_point(j):
+            for k in range(PAIRS):
+                i = 2 * k + j
+
+                def point(i=i):
+                    early_point(i)
+                    stage = i // 2 + 1
+                    if i % 2 == 1 and stage < stages - 1:
+                        gather(stage)
+
+                pl.when(p == k)(point)
+
+        dq = grad_pass(
+            own_rows(p), da_ext[p], da_ext[PAIRS],
+            lambda i: qkv[3 + p, i, :], lambda i: qkv[6 + p, i, :], lambda i: augk[i, :],
+            p, pieces_n, split, chunk, False, at_point,
+        )
+        dqkv[p] = (dq * HEAD_DIM**-0.5).astype(BF16)
+        return carry
+
+    lax.fori_loop(0, PAIRS, query_pass, 0)
+    gather(stages - 1)
+
+    def key_pass(p, carry):
+        def at_point(j):
+            for k in range(PAIRS):
+                i = 2 * PAIRS + 2 * k + j
+
+                def point(i=i, k=k):
+                    early_point(i)
+                    for m in range(k):
+                        step = 2 * (k - m - 1) + j
+                        late[m].finish(step)
+                        late[m].start(step + 1)
+
+                pl.when(p == k)(point)
+
+        dk, dv = grad_pass(
+            own_rows(3 + p), own_rows(6 + p), own_augk,
+            lambda i: qkv[p, i, :], lambda i: dag[p, i, :], lambda i: dag[PAIRS, i, :],
+            p, pieces_n, split, chunk, True, at_point,
+        )
+        d = jnp.concatenate([dqkv[p], dk.astype(BF16), dv.astype(BF16)], axis=1)
+        buf[pl.ds(pl.multiple_of(EARLY + 384 * p, 128), 384), :] = tn(h1_scr[...], d).astype(BF16)
+        w = jnp.concatenate(
+            [w_qkv[:, pl.ds(pl.multiple_of(384 * b + 128 * p, 128), 128)] for b in range(3)], axis=1
+        )
+        dh1_scr[...] += nt(d, w)
+        for k in range(PAIRS - 1):
+            pl.when(p == k)(lambda k=k: late[k].start(0))
+        return carry
+
+    lax.fori_loop(0, PAIRS, key_pass, 0)
+    dx, dg = norm_back(*normed(x), dh1_scr[...], g_attn[...].reshape(1, -1))
+    buf[EARLY + 1152 : EARLY + 1168, :] = jnp.concatenate([dg, jnp.zeros((15, 384), F32)], axis=0).astype(BF16)
+    late[2].start(0)
+    dx = dx + dx2[...]
+    for k in range(2):
+        tail = jnp.concatenate([learned[k], jnp.zeros((rows - cells - MAPS, 384), F32)], axis=0)
+        whole = jnp.concatenate([dx[k * rows : k * rows + cells, :], tail], axis=0)
+
+        @pl.when(mine == k)
+        def _():
+            own_tok[...] = whole
+
+        @pl.when(mine != k)
+        def _():
+            tok_send[...] = whole.astype(BF16)
+
+    tok_copy = rc(tok_send, tok_land, tsem.at[0], tsem.at[1], (fi + half * (1 - 2 * mine), si))
     tok_copy.start()
-    n_early = early.shape[0]
-    buf[0:n_early, :] = early[...]
-    buf[n_early:, :] = late[...]
-    third = 1536
-    plan = []
-    starts = [(0, third), (third, third), (2 * third, 512), (n_early, 1536)]
-    for k, (start, length) in enumerate(starts):
-        r = k % len(rest)
-        plan.append((start, length, [("frame", 1)] + rest[r:] + rest[:r]))
-    steps = len(everyone)
-    halvings = min(5, steps)
-    state = []
-    at = 0
-    for start, length, order in plan:
-        state.append({"seg": start, "len": length, "land": at, "order": order, "hist": []})
-        at += length + (steps - halvings) * (length >> halvings)
-    sem = [0]
-
-    def next_sem():
-        sem[0] += 1
-        return sem[0] - 1
-
-    def ds(start, n):
-        return pl.ds(pl.multiple_of(start, CH), n)
-
-    for step in range(steps):
-        flying = []
-        for st in state:
-            axis, bit = st["order"][step]
-            c = coord(axis, bit, fi, si)
-            k = next_sem()
-            if step < halvings:
-                n = st["len"] // 2
-                keep, give = st["seg"] + c * n, st["seg"] + (1 - c) * n
-            else:
-                n = st["len"]
-                keep = give = st["seg"]
-            cp = rc(buf.at[ds(give, n), :], land.at[pl.ds(st["land"], n), :], send.at[k], recv.at[k], neighbour(axis, bit, fi, si))
-            cp.start()
-            flying.append((cp, keep, n))
-        for st, (cp, keep, n) in zip(state, flying):
-            cp.wait()
-            at = st["land"]
-
-            def add(i, carry, keep=keep, at=at):
-                there = ds(keep + i * CH, CH)
-                buf[there, :] = (buf[there, :].astype(F32) + land[ds(at + i * CH, CH), :].astype(F32)).astype(BF16)
-                return carry
-
-            lax.fori_loop(0, n // CH, add, 0)
-            st["hist"].append((st["seg"], st["len"]))
-            st["seg"], st["len"], st["land"] = keep, n, at + n
-    for st in state:
-        out[ds(st["seg"], st["len"]), :] = buf[ds(st["seg"], st["len"]), :]
-    for step in reversed(range(halvings)):
-        flying = []
-        for st in state:
-            axis, bit = st["order"][step]
-            k = next_sem()
-            there = out.at[ds(st["seg"], st["len"]), :]
-            cp = rc(there, there, send.at[k], recv.at[k], neighbour(axis, bit, fi, si))
-            cp.start()
-            flying.append(cp)
-        for st, cp in zip(state, flying):
-            cp.wait()
-            st["seg"], st["len"] = st["hist"][step]
-    early_out[...] = out[0:n_early, :].astype(F32)
-    late_out[...] = out[n_early:, :].astype(F32)
+    used = 4 * PAIRS
+    done = [2 * (PAIRS - 1 - m) for m in range(PAIRS)]
+    for i in range(max(max(p.total for p in early) - used, max(p.total - n for p, n in zip(late, done)))):
+        early_point(used + i)
+        for piece, n in zip(late, done):
+            piece.finish(n + i)
+            piece.start(n + i + 1)
+    give = pltpu.make_async_copy(out, sums, fsem.at[0])
+    give.start()
     tok_copy.wait()
-    far = tok_land[...].astype(F32)
-    dtok_out[mine] = dtok[mine][0:cells, :]
-    dtok_out[1 - mine] = far[0:cells, :]
-    learned_out[mine] = dtok[mine][cells : cells + MAPS, :]
-    learned_out[1 - mine] = far[cells : cells + MAPS, :]
+    far_tok[...] = tok_land[...]
+    give.wait()
+
+
+def finish_kernel(cells, half, sums, own_tok, far_tok, d_tokens, learned, g_attn, w_qkv, w_out, g_mlp, w_up, w_down, g_learn, first, rest):
+    for j in range(4):
+        w_up[:, 384 * j : 384 * j + 384] = sums[384 * j : 384 * j + 384, :].astype(F32)
+    w_down[...] = sums[1536:3072, :].astype(F32)
+    w_out[...] = sums[3072:3456, :].astype(F32)
+    small = sums[3456:3584, :].astype(F32)
+    first[...] = small[0:72]
+    rest[...] = small[80:104, 0:128]
+    g_mlp[...] = small[72:73].reshape(-1)
+    g_learn[...] = small[73:74].reshape(-1)
+    for p in range(PAIRS):
+        block = sums[EARLY + 384 * p : EARLY + 384 * p + 384, :].astype(F32)
+        for b in range(3):
+            w_qkv[:, 384 * b + 128 * p : 384 * b + 128 * p + 128] = block[:, 128 * b : 128 * b + 128]
+    g_attn[...] = sums[EARLY + 1152 : EARLY + 1168, :].astype(F32)[0:1].reshape(-1)
+    mine = lax.axis_index("frame") // half
+    far = far_tok[...].astype(F32)
+    near = own_tok[...]
+    d_tokens[mine] = near[0:cells]
+    d_tokens[1 - mine] = far[0:cells]
+    learned[mine] = near[cells : cells + MAPS]
+    learned[1 - mine] = far[cells : cells + MAPS]
 
 
 def vspec(n):
@@ -749,7 +894,7 @@
     )(jnp.pad(tokens, ((0, 0), (0, rows - cells), (0, 0))), segments, d_learned.astype(F32))
     first9 = conv_first.transpose(1, 2, 0, 3).reshape(9, MAPS, width).astype(F32)
     rest27 = conv_rest.transpose(0, 2, 3, 1, 4).reshape(27, MAPS, MAPS).astype(F32)
-    qkv, augk, da_ext, dx2, learned, early = pl.pallas_call(
+    qkv, augk, da_ext, dx2, learned, early, own_x = pl.pallas_call(
         functools.partial(layer_kernel, frames, rows, cells),
         out_shape=[
             sds((9, total, 128), BF16),
@@ -757,10 +902,11 @@
             sds((PAIRS + 1, own, 128), BF16),
             sds((own, width), F32),
             sds((2, MAPS, width), F32),
-            sds((3584, width), BF16),
+            sds((EARLY, width), BF16),
+            sds((2, rows, width), BF16),
         ],
         in_specs=vspec(12),
-        out_specs=vspec(6),
+        out_specs=vspec(7),
         scratch_shapes=[
             VMEM((own, 128), F32),
             VMEM((PAIRS, own, 128), F32),
@@ -792,68 +938,62 @@
         xg, g_attn, w_qkv, w_out, g_mlp, w_up, w_down, g_learn, first9, rest27,
         jnp.asarray(tap_masks()), jnp.asarray(head_sums()),
     )
-    dag = pl.pallas_call(
-        functools.partial(da_gather_kernel, frames, rows),
-        out_shape=sds((PAIRS + 1, total, 128), BF16),
-        in_specs=vspec(1),
-        out_specs=vspec(1)[0],
+    n_all = EARLY + LATE
+    steps = 1 + len(mesh_bits(frames, seqs))
+    land_n = sum(landing_rows(n, steps, EARLY_HALVINGS) for _, n in EARLY_CUTS)
+    land_n += sum(landing_rows(n, steps, LATE_HALVINGS) for _, n in LATE_CUTS)
+    anywhere = pl.BlockSpec(memory_space=pl.ANY)
+    sums, own_tok, far_tok = pl.pallas_call(
+        functools.partial(back_kernel, frames, seqs, rows, cells),
+        out_shape=[sds((n_all, width), BF16), sds((rows, width), F32), sds((rows, width), BF16)],
+        in_specs=[anywhere] * 3 + vspec(6),
+        out_specs=[anywhere] + vspec(2),
         scratch_shapes=[
+            VMEM((9, total, 128), BF16),
+            VMEM((total, 128), BF16),
             VMEM((PAIRS + 1, total, 128), BF16),
-            pltpu.SemaphoreType.DMA((n_sems,)),
-            pltpu.SemaphoreType.DMA((frames,)),
-        ],
-        compiler_params=params(1),
-        name="grads_to_half",
-    )(da_ext)
-    dtok, late = pl.pallas_call(
-        functools.partial(back_kernel, frames, rows, cells),
-        out_shape=[sds((2, rows, width), F32), sds((1536, width), BF16)],
-        in_specs=vspec(9),
-        out_specs=vspec(2),
-        scratch_shapes=[VMEM((9, own, 128), BF16)],
-        compiler_params=params(),
-        name="attention_back",
-    )(qkv, augk, da_ext, dag, dx2, xg, g_attn, w_qkv, learned)
-    n_all = 3584 + 1536
-    early_sum, late_sum, d_tokens, learned_all = pl.pallas_call(
-        functools.partial(sum_kernel, frames, seqs, rows, cells),
-        out_shape=[
-            sds((3584, width), F32),
-            sds((1536, width), F32),
-            sds((2, cells, width), F32),
-            sds((2, MAPS, width), F32),
-        ],
-        in_specs=vspec(3),
-        out_specs=vspec(4),
-        scratch_shapes=[
+            VMEM((PAIRS, own, 128), BF16),
+            VMEM((own, width), BF16),
+            VMEM((own, width), F32),
             VMEM((n_all, width), BF16),
-            VMEM((n_all + (n_all >> 5) * max(0, len(mesh_bits(frames, seqs)) - 4), width), BF16),
+            VMEM((land_n, width), BF16),
             VMEM((n_all, width), BF16),
             VMEM((rows, width), BF16),
             VMEM((rows, width), BF16),
-            pltpu.SemaphoreType.DMA((64,)),
-            pltpu.SemaphoreType.DMA((64,)),
+            pltpu.SemaphoreType.DMA((3,)),
+            pltpu.SemaphoreType.DMA((n_sems,)),
+            pltpu.SemaphoreType.DMA((frames,)),
+            pltpu.SemaphoreType.DMA((12 * steps,)),
+            pltpu.SemaphoreType.DMA((12 * steps,)),
             pltpu.SemaphoreType.DMA((2,)),
         ],
-        compiler_params=params(2),
-        name="sums",
-    )(early, late, dtok)
-    d_w_up = jnp.concatenate([early_sum[384 * j : 384 * j + 384] for j in range(4)], axis=1)
-    d_w_qkv = jnp.concatenate([late_sum[384 * j : 384 * j + 384] for j in range(3)], axis=1)
-    d_first = early_sum[3456 : 3456 + 72].reshape(3, 3, MAPS, width).transpose(2, 0, 1, 3)
-    d_rest = early_sum[3536 : 3536 + 24, :72].reshape(3, MAPS, 3, 3, MAPS)
+        compiler_params=params(1),
+        name="attention_back",
+    )(qkv, augk, early, da_ext, dx2, own_x, g_attn, w_qkv, learned)
+    d_tokens, learned_all, dg_attn, d_w_qkv, d_w_out, dg_mlp, d_w_up, d_w_down, dg_learn, first, rest = pl.pallas_call(
+        functools.partial(finish_kernel, cells, frames // 2),
+        out_shape=[
+            sds((2, cells, width), F32),
+            sds((2, MAPS, width), F32),
+            sds((width,), F32),
+            sds((width, 3 * width), F32),
+            sds((width, width), F32),
+            sds((width,), F32),
+            sds((width, 4 * width), F32),
+            sds((4 * width, width), F32),
+            sds((width,), F32),
+            sds((72, width), F32),
+            sds((24, 128), F32),
+        ],
+        in_specs=vspec(3),
+        out_specs=vspec(11),
+        compiler_params=params(),
+        name="outputs",
+    )(sums, own_tok, far_tok)
+    d_first = first.reshape(3, 3, MAPS, width).transpose(2, 0, 1, 3)
+    d_rest = rest[:, :72].reshape(3, MAPS, 3, 3, MAPS)
     return (
-        learned_all.astype(BF16),
-        d_tokens,
-        late_sum[1152],
-        d_w_qkv,
-        early_sum[3072:3456],
-        early_sum[3528],
-        d_w_up,
-        early_sum[1536:3072],
-        early_sum[3529],
-        d_first,
-        d_rest,
+        learned_all.astype(BF16), d_tokens, dg_attn, d_w_qkv, d_w_out, dg_mlp, d_w_up, d_w_down, dg_learn, d_first, d_rest,
     )
 
 

time: 246 us -> 198 us (0.80)
  Pallas kernels: 222 us -> 186 us
  local copies, waits for them, and re-layouts: 14.3 us -> 5.44 us
  other arithmetic: 8.62 us -> 5.59 us
    pallas_call x3 -> x2, Pallas kernels: 144 us -> 108 us  [the longest x1 102 us: on_device(): pl.pallas_call(functools.partial(back_kernel, frames, seqs, rows, cells),...]
    slice x5 -> x0, local copies, waits for them, and re-layouts: 9.44 us -> none  [the longest x1 3.22 us: on_device(): early_sum[1536:3072]]
    concatenate x2 -> x0, other arithmetic: 3.03 us -> none  [the longest x1 1.71 us: on_device(): jnp.concatenate([early_sum[384 * j:384 * j + 384] for j in range(4)], axi...]
where the time goes in v2:
time: 198 us
  Pallas kernels  186 us (94%)
  other arithmetic  5.59 us (3%)
  local copies, waits for them, and re-layouts  5.44 us (3%)
    pallas_call x1, Pallas kernels, on_device(): pl.pallas_call(functools.partial(back_kernel, frames, seqs, rows, cells),...  102 us
    pallas_call x1, Pallas kernels, on_device(): pl.pallas_call(functools.partial(layer_kernel, frames, rows, cells), out_...  51 us
    pallas_call x1, Pallas kernels, on_device(): pl.pallas_call(functools.partial(token_gather_kernel, frames, cells), out...  27.2 us
    pallas_call x1, Pallas kernels, on_device(): pl.pallas_call(functools.partial(finish_kernel, cells, frames // 2), out_...  5.53 us

profile of v2, /device:TPU:0, one launch (start us, length us, event | category | flops | bytes accessed | tf_op | source)
XLA Modules:
  0.0 197.8 jit_solution(12361847400635247681)
XLA Ops:
  0.6 1.3 convert_element_type.22.d_learned
  2.0 1.5 convert_element_type.32
  3.4 1.5 convert_element_type.33
  4.9 1.0 copy.28
  5.9 0.8 pad.4.tokens
  6.7 27.2 %tokens_to_half.1.xg = bf16[16,208,384]{2,1,0:T(8,128)(2,1)} custom-call(bf16[2,208,384]{2,1,0:T(8,128)(2,1)} %pad.4.tokens, s32[2,196]{1,0:T(2,128)} %segments.1, f32[2,8,384]{2,1,0:T(8,128)} %convert_element_type.22.d_learned), custom_call_target="tpu_custom_call" | custom-call | tf_op jit(solution)/shard_map/tokens_to_half/pallas_call | solution.py:881
  33.9 51.0 %layer.1 = (bf16[9,3328,128]{2,1,0:T(8,128)(2,1)}, bf16[3328,128]{1,0:T(8,128)(2,1)}, bf16[4,416,128]{2,1,0:T(8,128)(2,1)}, f32[416,384]{1,0:T(8,128)}, f32[2,8,...) custom-call(bf16[16,208,384]{2,1,0:T(8,128)(2,1)} %tokens_to_half.1.xg, f32[384]{0:T(512)} %g_attn.3, ...), custom_call_target="tpu_custom_call" | custom-call | tf_op jit(solution)/shard_map/layer/pallas_call | solution.py:897
  84.9 102.4 %attention_back.1 = (bf16[4864,384]{1,0:T(8,128)(2,1)}, f32[208,384]{1,0:T(8,128)}, bf16[208,384]{1,0:T(8,128)(2,1)}) custom-call(bf16[9,3328,128]{2,1,0:T(8,128)(2,1)} %get-tuple-element.32.qkv_hbm, bf16[3328,128]{1,0:T(8,128)(2,1)} %get-tuple-element.33.augk_hbm, bf16[3584,384]{1,0:T(8,128)(2,1)} %get-tuple-element.34.early_hbm, ...), custom_call_target="tpu_custom_call" | custom-call | tf_op jit(solution)/shard_map/attention_back/pallas_call | solution.py:946
  187.3 5.5 %outputs.1 = (f32[2,196,384]{2,1,0:T(8,128)}, f32[2,8,384]{2,1,0:T(8,128)}, f32[384]{0:T(512)}, f32[384,1152]{1,0:T(8,128)}, f32[384,384]{1,0:T(8,128)}, /*index...) custom-call(bf16[4864,384]{1,0:T(8,128)(2,1)} %get-tuple-element.39., ...), custom_call_target="tpu_custom_call" | custom-call | tf_op jit(solution)/shard_map/outputs/pallas_call | solution.py:973
  192.8 1.3 convert_element_type.29
  194.2 0.8 reshape.35
  195.0 0.7 copy.30
  195.6 2.2 %copy.29 = f32[2,196,384]{2,0,1:T(2,128)} copy(f32[2,196,384]{2,1,0:T(8,128)} %get-tuple-element.65) | data formatting | bytes 1204224

commit v3 on v2

v3 whole, which is shorter than its diff:
```python
import functools

import jax
import jax.numpy as jnp
import numpy as np
from jax import lax
from jax.experimental import pallas as pl
from jax.experimental.pallas import tpu as pltpu
from jax.sharding import PartitionSpec as P

HEADS = 6
HEAD_DIM = 64
MAPS = 8
GRID = 14
CELLS = GRID * GRID
PAIRS = HEADS // 2
WIDE = 512
BIG = 1e30
LSE0 = 4
DEL0 = 4 + 3 * HEADS
AUG_END = 4 + 6 * HEADS
F32 = jnp.float32
BF16 = jnp.bfloat16
HIGH = lax.Precision.HIGHEST
MESH = pl.DeviceIdType.MESH
VMEM = pltpu.VMEM
MIB = 1 << 20


def nn(a, b, precision=None):
    return lax.dot_general(a, b, (((1,), (0,)), ((), ())), precision=precision, preferred_element_type=F32)


def nt(a, b, precision=None):
    return lax.dot_general(a, b, (((1,), (1,)), ((), ())), precision=precision, preferred_element_type=F32)


def tn(a, b, precision=None):
    return lax.dot_general(a, b, (((0,), (0,)), ((), ())), precision=precision, preferred_element_type=F32)


def iota(shape, dim):
    return lax.broadcasted_iota(jnp.int32, shape, dim)


def sixteen(v):
    return jnp.concatenate([v, jnp.zeros((8, v.shape[1]), v.dtype)], axis=0)


def normed(x):
    centered = x - jnp.mean(x, axis=-1, keepdims=True)
    rstd = lax.rsqrt(jnp.mean(centered * centered, axis=-1, keepdims=True) + 1e-06)
    return centered * rstd, rstd


def norm_back(vhat, rstd, dout, gain):
    e = dout * gain
    mean_e = jnp.mean(e, axis=-1, keepdims=True)
    mean_ev = jnp.mean(e * vhat, axis=-1, keepdims=True)
    return rstd * (e - mean_e - vhat * mean_ev), jnp.sum(dout * vhat, axis=0, keepdims=True)


C0 = 0.7978845608028654
C1 = 0.044715


def gelu(u):
    return 0.5 * u * (1.0 + jnp.tanh(C0 * (u + C1 * u * u * u)))


def gelu_grad(u):
    t = jnp.tanh(C0 * (u + C1 * u * u * u))
    return 0.5 * (1.0 + t) + 0.5 * u * (1.0 - t * t) * (C0 + (3.0 * C0 * C1) * u * u)


def flip(v, b):
    return v + b * (1 - 2 * ((v // b) % 2))


def bit_of(v, b):
    return (v // b) % 2


def rc(src, dst, send, recv, dev):
    return pltpu.make_async_remote_copy(
        src_ref=src, dst_ref=dst, send_sem=send, recv_sem=recv, device_id=dev, device_id_type=MESH
    )


def greet(partners):
    barrier = pltpu.get_barrier_semaphore()
    for dev in partners:
        pl.semaphore_signal(barrier, inc=1, device_id=dev, device_id_type=MESH)
    pl.semaphore_wait(barrier, len(partners))


class Gather:
    def __init__(self, half, base, turn, block, send, recv, first, fi, si):
        self.g, self.base, self.block, self.send, self.recv = fi % half, base, block, send, recv
        self.fi, self.si = fi, si
        bits = []
        b = 2
        while b < half:
            bits.append(b)
            b *= 2
        n = len(bits)
        self.n = n
        self.order = bits[turn % n :] + bits[: turn % n] if n else []
        self.pushes = [[] for _ in range(n + 2)]
        count = first
        for stage in range(n + 1):
            for j in range(1 << max(stage - 1, 0)):
                for bit in self.order[stage:] + [1]:
                    self.pushes[stage].append((stage, j, count, bit))
                    count += 1
        self.end = count
        self.last = n + 1

    def delta(self, bit):
        return bit * (1 - 2 * bit_of(self.g, bit))

    def arrivals(self, stage):
        return 1 << (self.n if stage == self.last else stage - 1)

    def slot(self, stage, j):
        at = self.base + self.g
        if stage == 0:
            return at
        passed = self.order if stage == self.last else self.order[: stage - 1]
        for k, bit in enumerate(passed):
            at = at + ((j // (1 << k)) % 2) * self.delta(bit)
        return at + self.delta(1 if stage == self.last else self.order[stage - 1])

    def copy(self, slot, k, bit):
        ref = self.block(slot)
        return rc(ref, ref, self.send.at[k], self.recv.at[slot], (flip(self.fi, bit), self.si))

    def run(self, stage):
        if stage > 0:
            for j in range(self.arrivals(stage)):
                slot = self.slot(stage, j)
                self.copy(slot, 0, 1).wait_recv()
                for st, i, k, bit in self.pushes[stage]:
                    if i == j:
                        self.copy(slot, k, bit).start()
        else:
            for st, i, k, bit in self.pushes[0]:
                self.copy(self.slot(0, 0), k, bit).start()

    def drain(self):
        for stage in self.pushes:
            for st, i, k, bit in stage:
                self.copy(self.slot(st, i), k, bit).wait_send()


def aug_masks(h):
    lane = iota((1, 128), 1)
    seg = lane < 4
    lse = seg | ((lane >= LSE0 + 3 * h) & (lane < LSE0 + 3 * h + 3))
    dlt = (lane >= DEL0 + 3 * h) & (lane < DEL0 + 3 * h + 3)
    return lse.astype(F32).astype(BF16), dlt.astype(F32).astype(BF16)


def pieces(value, which):
    hi = value.astype(BF16).astype(F32)
    rest = value - hi
    mid = rest.astype(BF16).astype(F32)
    low = rest - mid
    return jnp.where(which == 0, hi, jnp.where(which == 1, mid, low))


def half_masks():
    lane = iota((1, 128), 1)
    first = (lane < HEAD_DIM).astype(F32).astype(BF16)
    return first, (lane >= HEAD_DIM).astype(F32).astype(BF16)


def grad_pass(own_a, own_b, own_aug, all_a, all_b, all_aug, p, count, split, chunk, with_b, at_point):
    masks = half_masks()
    left_a, left_b = [], []
    for e in range(2):
        lse_mask, del_mask = aug_masks(2 * p + e)
        left_a.append(jnp.concatenate([own_a * masks[e], own_aug * lse_mask], axis=1))
        left_b.append(jnp.concatenate([own_b * masks[e], own_aug * del_mask], axis=1))
    acc = [jnp.zeros((own_a.shape[0], 128), F32) for _ in range(2 if with_b else 1)]
    for c in range(count):
        here = pl.ds(c * chunk, chunk)
        ra, rb, aug = all_a(here), all_b(here), all_aug(here)
        right_a = jnp.concatenate([ra, aug], axis=1)
        right_b = jnp.concatenate([rb, aug], axis=1)
        probs = [jnp.exp(nt(left_a[e], right_a)) for e in range(2)]
        ds = [(probs[e] * nt(left_b[e], right_b)).astype(BF16) for e in range(2)]
        acc[0] = acc[0] + nn(jnp.concatenate(ds, axis=1), jnp.concatenate([ra * m for m in masks], axis=0))
        if with_b:
            both = jnp.concatenate([prob.astype(BF16) for prob in probs], axis=1)
            acc[1] = acc[1] + nn(both, jnp.concatenate([rb * m for m in masks], axis=0))
        if c + 1 == split:
            at_point(0)
    at_point(1)
    return acc if with_b else acc[0]


def mesh_bits(frames, seqs):
    rest = []
    b = 1
    while b < seqs:
        rest.append(("seq", b))
        b *= 2
    b = 2
    while b < frames:
        rest.append(("frame", b))
        b *= 2
    return rest


TILE = 16


def at_tile(start, n):
    return pl.ds(start if isinstance(start, int) else pl.multiple_of(start, TILE), n)


def member(group, offset, fi, si):
    index = 0
    for i, (axis, bit) in enumerate(group):
        value = bit_of(fi if axis == "frame" else si, bit)
        if (offset >> i) & 1:
            value = 1 - value
            if axis == "frame":
                fi = flip(fi, bit)
            else:
                si = flip(si, bit)
        index = index + value * (1 << i)
    return (fi, si), index


def pairs_of(bits):
    return [bits[i : i + 2] for i in range(0, len(bits), 2)]


EARLY = 3584
LATE = 3 * 384 + 128
EARLY_CUTS = ((0, 1536), (1536, 2048))
LATE_CUTS = ((EARLY, 384), (EARLY + 384, 384), (EARLY + 768, 512))
EARLY_BITS = 5
LATE_BITS = 3


def early_groups(frames, seqs):
    rest = mesh_bits(frames, seqs)
    return [[("frame", 1)], rest[:1]] + pairs_of(rest[1:])


def late_groups(frames, seqs):
    return [[("frame", 1)]] + pairs_of(mesh_bits(frames, seqs))


def landing(length, groups, most_bits):
    rows = copies = bits = 0
    for group in groups:
        others = (1 << len(group)) - 1
        bits += len(group)
        copies += others
        if bits <= most_bits:
            length >>= len(group)
            copies += others
        rows += others * length
    return rows, copies


class Piece:
    def __init__(self, start, length, groups, most_bits, land_at, sem_at, fi, si, buf, land, out, send, recv):
        self.refs = buf, land, out, send, recv
        self.steps = []
        seg, n, sem, bits = start, length, sem_at, 0
        hist = []
        for group in groups:
            bits += len(group)
            offsets = range(1, 1 << len(group))
            moves = []
            if bits <= most_bits:
                hist.append((seg, n, group))
                n >>= len(group)
                _, index = member(group, 0, fi, si)
                for d in offsets:
                    dev, other = member(group, d, fi, si)
                    moves.append((seg + other * n, land_at, sem, dev))
                    land_at, sem = land_at + n, sem + 1
                seg = seg + index * n
            else:
                for d in offsets:
                    dev, _ = member(group, d, fi, si)
                    moves.append((seg, land_at, sem, dev))
                    land_at, sem = land_at + n, sem + 1
            self.steps.append(("add", seg, n, moves))
        self.adds = len(groups)
        for old, old_n, group in reversed(hist):
            moves = []
            for d in range(1, 1 << len(group)):
                moves.append((seg, 0, sem, member(group, d, fi, si)[0]))
                sem += 1
            self.steps.append(("copy", seg, n, moves))
            seg, n = old, old_n
        self.sem_end = sem
        self.land_end = land_at
        self.total = len(self.steps)

    def copies(self, i):
        buf, land, out, send, recv = self.refs
        kind, _, n, moves = self.steps[i]
        made = []
        for give, at, sem, dev in moves:
            src = (buf if kind == "add" else out).at[at_tile(give, n), :]
            dst = land.at[at_tile(at, n), :] if kind == "add" else src
            made.append(rc(src, dst, send.at[sem], recv.at[sem], dev))
        return made

    def start(self, i):
        if i < self.total:
            for cp in self.copies(i):
                cp.start()

    def finish(self, i):
        if i < 0 or i >= self.total:
            return
        buf, land, out, _, _ = self.refs
        for cp in self.copies(i):
            cp.wait()
        kind, keep, n, moves = self.steps[i]
        if kind == "copy":
            return
        to = out if i == self.adds - 1 else buf
        chunk = max(TILE * k for k in (1, 2, 3, 4, 6, 7) if n % (TILE * k) == 0)

        def add(j, carry):
            here = at_tile(keep + j * chunk, chunk)
            value = buf[here, :].astype(F32)
            for _, at, _, _ in moves:
                value = value + land[at_tile(at + j * chunk, chunk), :].astype(F32)
            to[here, :] = value.astype(BF16)
            return carry

        lax.fori_loop(0, n // chunk, add, 0)


def partners_of(all_groups, fi, si):
    seen, devs = set(), []
    for groups in all_groups:
        for group in groups:
            for d in range(1, 1 << len(group)):
                key = tuple(sorted(group[i] for i in range(len(group)) if (d >> i) & 1))
                if key not in seen:
                    seen.add(key)
                    devs.append(member(group, d, fi, si)[0])
    return devs


EARLY_POINTS = ((2, 5, 6, 7, 8, 10, 11), (4, 6, 7, 8, 9))


def whole_kernel(
    frames, seqs, rows, cells,
    tokens, segments, d_learned, g_attn, w_qkv, w_out, g_mlp, w_up, w_down, g_learn, first9, rest27, tapmask, blockones,
    sums, own_tok, far_tok,
    xp, xg, qkv, augk, dag, da_ext, dx2_scr, learned,
    augq, o_scr, x2_scr, y_scr, vhat2_scr, vhat3_scr, rstd2_scr, rstd3_scr,
    dh2_scr, u_scr, h3p, yp,
    dyp, w72_scr, spread_scr, rest_scr, gain_scr, conv_bw, conv_fw, dqkv,
    h1_scr, dh1_scr, buf, land, out, tok_send, tok_land, tsend,
    trecv, gsend, grecv, psend, precv, fsem, tsem,
):
    fi = lax.axis_index("frame")
    si = lax.axis_index("seq")
    half = frames // 2
    g = fi % half
    mine = fi // half
    total = frames * rows
    own = 2 * rows
    other = fi + half * (1 - 2 * mine)
    partner = (other, si)
    for k in range(2):
        body = tokens[k].astype(F32)[0:cells]
        seg = jnp.broadcast_to(segments[k : k + 1, 0:1].astype(F32), (1, 384))
        pad = jnp.zeros((rows - cells - 1 - MAPS, 384), F32)
        xp[k] = jnp.concatenate([body, seg, d_learned[k], pad], axis=0).astype(BF16)
    xg[fi] = xp[mine]
    singles = [[bit] for bit in mesh_bits(frames, seqs)]
    by_early, by_late = early_groups(frames, seqs), late_groups(frames, seqs)
    greet(partners_of((singles, by_early, by_late), fi, si))
    token_block = lambda slot: xg.at[slot]
    near = Gather(half, half * mine, 0, token_block, tsend, trecv, 1, fi, si)
    far = Gather(half, half * (1 - mine), 1, token_block, tsend, trecv, near.end, fi, si)
    to_partner = rc(xp.at[1 - mine], xg.at[fi], tsend.at[0], trecv.at[fi], partner)
    to_partner.start()
    near.run(0)
    da_block = lambda slot: dag.at[:, pl.ds(pl.multiple_of(slot * rows, rows), rows), :]
    da_near = Gather(half, 0, 0, da_block, gsend, grecv, 0, fi, si)
    da_far = Gather(half, half, 1, da_block, gsend, grecv, da_near.end, fi, si)
    refs = fi, si, buf, land, out, psend, precv
    early, late = [], []
    land_at = sem_at = 0
    for group, cuts, by, bits in ((early, EARLY_CUTS, by_early, EARLY_BITS), (late, LATE_CUTS, by_late, LATE_BITS)):
        for start, length in cuts:
            group.append(Piece(start, length, by, bits, land_at, sem_at, *refs))
            land_at, sem_at = group[-1].land_end, group[-1].sem_end

    h2_rows, a_rows, dm_rows = (pl.ds(own * k, own) for k in (4, 5, 6))

    def early_point(i):
        for piece, points in zip(early, EARLY_POINTS):
            if i in points:
                step = 1 + points.index(i)
                piece.finish(step)
                piece.start(step + 1)

    lane128 = iota((rows, 128), 1)
    row128 = iota((rows, 128), 0)
    valid_row = row128 < cells

    w72 = first9[...].reshape(72, 384)
    w72_scr[...] = sixteen(w72).astype(BF16)
    square_r, square_c = iota((128, 128), 0), iota((128, 128), 1)
    repeat = ((square_c & 7) == square_r).astype(F32)
    same_tap = (((square_r >> 3) == (square_c >> 3)) & (square_r < 72)).astype(F32)
    for layer in range(3):
        by_tap = rest27[9 * layer : 9 * layer + 9].reshape(72, MAPS)
        by_tap = jnp.concatenate([by_tap, jnp.zeros((72, 120), F32)], axis=1)
        conv_bw[layer] = sixteen(by_tap)
        by_tap = jnp.concatenate([by_tap, jnp.zeros((56, 128), F32)], axis=0)
        conv_fw[layer] = nn(repeat[0:16], nn(by_tap, repeat, HIGH) * same_tap, HIGH)

    def project(f, carry):
        x = xg[f].astype(F32)
        seg = x[cells : cells + 1, 0:128]
        x = jnp.where(iota(x.shape, 0) < cells, x, 0.0)
        vhat, _ = normed(x)
        h1 = (vhat * g_attn[...].reshape(1, -1)).astype(BF16)
        base = pl.multiple_of(f * rows, rows)
        whole = nn(h1, w_qkv[...])
        for b in range(9):
            part = whole[:, 128 * b : 128 * b + 128]
            if b < 3:
                part = part * HEAD_DIM**-0.5
            qkv[b, pl.ds(base, rows), :] = part.astype(BF16)
        same = (lane128.astype(F32) == seg) & valid_row
        augk[pl.ds(base, rows), :] = jnp.where(
            lane128 < 4, jnp.where(same, 0.0, -BIG), jnp.where(lane128 < AUG_END, -1.0, 0.0)
        ).astype(BF16)
        return carry

    def project_stage(gather, stage):
        gather.run(stage)
        if stage == 0:
            project(gather.slot(0, 0), 0)
        else:
            lax.fori_loop(0, gather.arrivals(stage), lambda j, c: project(gather.slot(stage, j), c), 0)

    project(near.slot(0, 0), 0)
    project_stage(near, 1)
    far_block = xg.at[other]
    rc(far_block, far_block, tsend.at[0], trecv.at[other], partner).wait_recv()
    project_stage(far, 0)
    for stage in range(2, near.last):
        project_stage(near, stage)
    for stage in range(1, near.last):
        project_stage(far, stage)
    project_stage(near, near.last)
    project_stage(far, far.last)
    to_partner.wait_send()
    near.drain()
    far.drain()

    ones = jnp.ones((frames * rows, 128), BF16)

    for k in range(2):
        f = g + half * k
        seg = xg[f].astype(F32)[cells : cells + 1, 0:128]
        same = (lane128.astype(F32) == seg) & valid_row & (lane128 < 4)
        augq[k * rows : (k + 1) * rows, :] = same.astype(F32)

    together = 2 if frames <= 16 else 1

    def attend(step, carry):
        p = step // (4 // together)
        k = step % 2
        f = g + half * k
        q = qkv[p, pl.ds(pl.multiple_of(f * rows, rows), rows), :]
        mine = pl.ds(pl.multiple_of(k * rows, rows), rows)
        aug = augq[mine, :]
        seg_aug = jnp.where(lane128 < 4, aug, 0.0).astype(BF16)
        keys = jnp.concatenate([qkv[3 + p], augk[...]], axis=1)
        values = jnp.concatenate([qkv[6 + p], ones], axis=1)
        mixed = o_scr[p, mine, :] if together == 1 else 0.0
        for n in range(together):
            e = n if together == 2 else (step // 2) % 2
            keep = (lane128 >= HEAD_DIM * e) & (lane128 < HEAD_DIM * (e + 1))
            s = nt(jnp.concatenate([q * keep.astype(F32).astype(BF16), seg_aug], axis=1), keys)
            top = jnp.max(s, axis=1, keepdims=True)
            prob = jnp.exp(s - top).astype(BF16)
            o = nn(prob, values)
            weight = o[:, 128:]
            mixed = jnp.where(keep, o[:, :128] / weight, mixed)
            lse = top + jnp.log(weight)
            which = lane128 - (LSE0 + 3 * (2 * p + e))
            aug = jnp.where((which >= 0) & (which < 3), pieces(lse, which), aug)
        augq[mine, :] = aug
        o_scr[p, mine, :] = mixed
        return carry

    lax.fori_loop(0, 4 * PAIRS // together, attend, 0)

    def apart(fn):
        pl.when(fi >= 0)(fn)

    @apart
    def _():
        a = jnp.concatenate([o_scr[p].astype(BF16) for p in range(PAIRS)], axis=1)
        out[a_rows, :] = a
        both = jnp.concatenate([xg[g], xg[g + half]], axis=0).astype(F32)
        r = iota(both.shape, 0)
        x = jnp.where((r < cells) | ((r >= rows) & (r < rows + cells)), both, 0.0)
        x2 = x + nn(a, w_out[...])
        x2_scr[...] = x2
        y_scr[...] = x2
        vhat, rstd = normed(x2)
        rstd2_scr[...] = jnp.broadcast_to(rstd, (own, 128))
        vhat2_scr[...] = vhat
        out[h2_rows, :] = (vhat * g_mlp[...].reshape(1, -1)).astype(BF16)

    def mlp(j, carry):
        cols = pl.ds(pl.multiple_of(384 * j, 384), 384)
        u = nn(out[h2_rows, :], w_up[:, cols])
        u_scr[j] = u
        hid = gelu(u).astype(BF16)
        out[pl.ds(pl.multiple_of(own * j, 16), own), :] = hid
        y_scr[...] += nn(hid, w_down[cols, :])
        return carry

    lax.fori_loop(0, 4, mlp, 0)

    @apart
    def _():
        y = y_scr[...]
        vhat, rstd = normed(y)
        vhat3_scr[...] = vhat
        rstd3_scr[...] = jnp.broadcast_to(rstd, (own, 128))
        h3 = (vhat * g_learn[...].reshape(1, -1)).astype(BF16)
        for k in range(2):
            yp[256 * k : 256 * k + rows, :] = y[k * rows : (k + 1) * rows, :]
            yp[256 * k + rows : 256 * k + 256, :] = jnp.zeros((256 - rows, 384), F32)
            h3p[256 * k : 256 * k + rows, :] = h3[k * rows : (k + 1) * rows, :]
            h3p[256 * k + rows : 256 * k + 256, :] = jnp.zeros((256 - rows, 384), BF16)

    def shift_of(t):
        return GRID * (t // 3 - 1) + (t % 3 - 1)

    def moved(v, s):
        return v if s == 0 else pltpu.roll(v, (-s) % WIDE, 1)

    def tap(t):
        return tapmask[t : t + 1, :]

    def im2col(v):
        parts = [moved(v, shift_of(t)) * tap(t) for t in range(9)]
        return jnp.concatenate(parts + [jnp.zeros((56, WIDE), F32)], axis=0)

    def spread_of(v):
        return jnp.concatenate([moved(v, -shift_of(t)) * tap(8 - t) for t in range(9)], axis=0)

    @apart
    def _():
        taps = nt(w72_scr[...], h3p[...])
        z1 = jnp.zeros((MAPS, WIDE), F32)
        for t in range(9):
            z1 = z1 + moved(taps[8 * t : 8 * t + 8, :], shift_of(t)) * tap(t)
        zs = [z1]
        cols_of = []
        for layer in range(3):
            col = im2col(gelu(zs[-1]))
            cols_of.append(col)
            zs.append(nn(conv_fw[layer], col, HIGH)[0:MAPS])
        maps = tap(4) / (1.0 + jnp.exp(-zs[3]))
        dmaps = []
        for k in range(2):
            f = g + half * k
            dl = xg[f].astype(F32)[cells + 1 : cells + 1 + MAPS, :] * (1.0 / cells)
            dl = sixteen(dl)
            mk = sixteen(maps[:, 256 * k : 256 * k + 256])
            yk = yp[256 * k : 256 * k + 256, :]
            learned[k] = nn(mk, yk, HIGH)[0:MAPS] * (1.0 / cells)
            dmaps.append(nt(dl, yk, HIGH)[0:MAPS])
            dyp[256 * k : 256 * k + 256, :] = tn(mk, dl, HIGH)
        dz = jnp.concatenate(dmaps, axis=1) * maps * (1.0 - maps)
        small = []
        for layer in (2, 1, 0):
            dw = nt(sixteen(dz), cols_of[layer], HIGH)[0:MAPS]
            small.insert(0, jnp.concatenate([dw, jnp.zeros((MAPS, 256), F32)], axis=1))
            dz = tn(conv_bw[layer], sixteen(spread_of(dz)), HIGH)[0:MAPS] * gelu_grad(zs[layer])
        dz = dz.astype(BF16).astype(F32) * tap(4)
        spread_scr[...] = sixteen(spread_of(dz)).astype(BF16)
        rest_scr[...] = jnp.concatenate(small + [jnp.zeros((8, 384), F32)], axis=0)

    @apart
    def _():
        dh3 = tn(spread_scr[...], w72_scr[...])
        dh3 = jnp.concatenate([dh3[0:rows], dh3[256 : 256 + rows]], axis=0)
        dy, dg3 = norm_back(vhat3_scr[...], rstd3_scr[:, 0:1], dh3, g_learn[...].reshape(1, -1))
        dy = dy + jnp.concatenate([dyp[0:rows, :], dyp[256 : 256 + rows, :]], axis=0)
        y_scr[...] = dy
        out[dm_rows, :] = dy.astype(BF16)
        dh2_scr[...] = jnp.zeros((own, 384), F32)
        gain_scr[...] = jnp.concatenate([dg3, jnp.zeros((7, 384), F32)], axis=0)

    def mlp_back(j, carry):
        cols = pl.ds(pl.multiple_of(384 * j, 384), 384)
        dm = out[dm_rows, :]
        du = (nt(dm, w_down[cols, :]) * gelu_grad(u_scr[j])).astype(BF16)
        buf[cols, :] = tn(out[h2_rows, :], du).astype(BF16)
        buf[pl.ds(pl.multiple_of(1536 + 384 * j, 384), 384), :] = tn(out[pl.ds(pl.multiple_of(own * j, 16), own), :], dm).astype(BF16)
        dh2_scr[...] += nt(du, w_up[:, cols])
        return carry

    lax.fori_loop(0, 4, mlp_back, 0)
    early[0].start(0)

    @apart
    def _():
        dx2, dg2 = norm_back(vhat2_scr[...], rstd2_scr[:, 0:1], dh2_scr[...], g_mlp[...].reshape(1, -1))
        dx2 = dx2 + y_scr[...]
        dx2_scr[...] = dx2
        out[dm_rows, :] = dx2.astype(BF16)
        gains = jnp.concatenate([dg2, gain_scr[0:1, :], jnp.zeros((6, 384), F32)], axis=0)
        d_first = nn(spread_scr[...], h3p[...])[0:72]
        small = [d_first, gains, rest_scr[...], jnp.zeros((16, 384), F32)]
        buf[3456:3584, :] = jnp.concatenate(small, axis=0).astype(BF16)

    early[0].finish(0)
    early[0].start(1)

    @apart
    def _():
        dzz = out[dm_rows, :]
        buf[3072:3456, :] = tn(out[a_rows, :], dzz).astype(BF16)
        da = nt(dzz, w_out[...]).astype(BF16)
        prod = jnp.concatenate([o_scr[p] for p in range(PAIRS)], axis=1) * da.astype(F32)
        lane = iota((own, 128), 1)
        which = lane - DEL0
        which = which - 3 * (which // 3)
        delta = pieces(nn(prod, blockones[...], HIGH), which)
        full = jnp.where((lane >= DEL0) & (lane < AUG_END), delta, augq[...])
        full = full.astype(BF16)
        for p in range(PAIRS):
            da_ext[p] = da[:, 128 * p : 128 * p + 128]
        da_ext[PAIRS] = full
        for k in range(2):
            there = pl.ds(pl.multiple_of((g + half * k) * rows, rows), rows)
            dag[:, there, :] = da_ext[:, k * rows : (k + 1) * rows, :]

    early[1].start(0)
    da_near.run(0)
    da_far.run(0)
    x = jnp.concatenate([xg[g], xg[g + half]], axis=0).astype(F32)
    r = iota(x.shape, 0)
    x = jnp.where((r < cells) | ((r >= rows) & (r < rows + cells)), x, 0.0)
    vhat, _ = normed(x)
    h1_scr[...] = (vhat * g_attn[...].reshape(1, -1)).astype(BF16)
    dh1_scr[...] = jnp.zeros((own, 384), F32)
    buf[EARLY + 1152 :, :] = jnp.zeros((128, 384), BF16)
    early[1].finish(0)
    early[1].start(1)

    def own_rows(b):
        at = [qkv[b, pl.ds(pl.multiple_of((g + half * k) * rows, rows), rows), :] for k in range(2)]
        return jnp.concatenate(at, axis=0)

    own_augk = jnp.concatenate(
        [augk[pl.ds(pl.multiple_of((g + half * k) * rows, rows), rows), :] for k in range(2)], axis=0
    )
    chunk = 256
    pieces_n = total // chunk
    split = (pieces_n + 1) // 2

    def query_pass(p, carry):
        def at_point(j):
            for k in range(PAIRS):
                i = 2 * k + j

                def point(i=i):
                    early_point(i)
                    stage = i // 2 + 1
                    if i % 2 == 1 and stage < da_near.last:
                        da_near.run(stage)
                        da_far.run(stage)

                pl.when(p == k)(point)

        dq = grad_pass(
            own_rows(p), da_ext[p], da_ext[PAIRS],
            lambda i: qkv[3 + p, i, :], lambda i: qkv[6 + p, i, :], lambda i: augk[i, :],
            p, pieces_n, split, chunk, False, at_point,
        )
        dqkv[p] = (dq * HEAD_DIM**-0.5).astype(BF16)
        return carry

    lax.fori_loop(0, PAIRS, query_pass, 0)
    for gather in (da_near, da_far):
        gather.run(gather.last)
        gather.drain()

    def key_pass(p, carry):
        def at_point(j):
            for k in range(PAIRS):
                i = 2 * PAIRS + 2 * k + j

                def point(i=i, k=k):
                    early_point(i)
                    for m in range(k):
                        step = 2 * (k - m - 1) + j
                        late[m].finish(step)
                        late[m].start(step + 1)

                pl.when(p == k)(point)

        dk, dv = grad_pass(
            own_rows(3 + p), own_rows(6 + p), own_augk,
            lambda i: qkv[p, i, :], lambda i: dag[p, i, :], lambda i: dag[PAIRS, i, :],
            p, pieces_n, split, chunk, True, at_point,
        )
        d = jnp.concatenate([dqkv[p], dk.astype(BF16), dv.astype(BF16)], axis=1)
        buf[pl.ds(pl.multiple_of(EARLY + 384 * p, 128), 384), :] = tn(h1_scr[...], d).astype(BF16)
        w = jnp.concatenate(
            [w_qkv[:, pl.ds(pl.multiple_of(384 * b + 128 * p, 128), 128)] for b in range(3)], axis=1
        )
        dh1_scr[...] += nt(d, w)
        for k in range(PAIRS - 1):
            pl.when(p == k)(lambda k=k: late[k].start(0))
        return carry

    lax.fori_loop(0, PAIRS, key_pass, 0)
    dx, dg = norm_back(*normed(x), dh1_scr[...], g_attn[...].reshape(1, -1))
    buf[EARLY + 1152 : EARLY + 1168, :] = jnp.concatenate([dg, jnp.zeros((15, 384), F32)], axis=0).astype(BF16)
    late[2].start(0)
    dx = dx + dx2_scr[...]
    for k in range(2):
        tail = jnp.concatenate([learned[k], jnp.zeros((rows - cells - MAPS, 384), F32)], axis=0)
        whole = jnp.concatenate([dx[k * rows : k * rows + cells, :], tail], axis=0)

        @pl.when(mine == k)
        def _():
            own_tok[...] = whole

        @pl.when(mine != k)
        def _():
            tok_send[...] = whole.astype(BF16)

    tok_copy = rc(tok_send, tok_land, tsem.at[0], tsem.at[1], (fi + half * (1 - 2 * mine), si))
    tok_copy.start()
    give = [
        pltpu.make_async_copy(out.at[pl.ds(at, n), :], sums.at[pl.ds(at, n), :], fsem.at[i])
        for i, (at, n) in enumerate((EARLY_CUTS[0], (EARLY_CUTS[1][0], EARLY + LATE - EARLY_CUTS[1][0])))
    ]
    running = [(piece, 1 + len(points)) for piece, points in zip(early, EARLY_POINTS)]
    running += [(piece, 2 * (PAIRS - 1 - m)) for m, piece in enumerate(late)]
    for piece, n in running[:1]:
        for i in range(n, piece.total):
            piece.finish(i)
            piece.start(i + 1)
    give[0].start()
    for i in range(max(piece.total - n for piece, n in running[1:])):
        for piece, n in running[1:]:
            piece.finish(n + i)
            piece.start(n + i + 1)
    give[1].start()
    tok_copy.wait()
    far_tok[...] = tok_land[...]
    for cp in give:
        cp.wait()


def finish_kernel(cells, half, sums, own_tok, far_tok, d_tokens, learned, g_attn, w_qkv, w_out, g_mlp, w_up, w_down, g_learn, first, rest):
    for j in range(4):
        w_up[:, 384 * j : 384 * j + 384] = sums[384 * j : 384 * j + 384, :].astype(F32)
    w_down[...] = sums[1536:3072, :].astype(F32)
    w_out[...] = sums[3072:3456, :].astype(F32)
    small = sums[3456:3584, :].astype(F32)
    first[...] = small[0:72]
    rest[...] = small[80:104, 0:128]
    g_mlp[...] = small[72:73].reshape(-1)
    g_learn[...] = small[73:74].reshape(-1)
    for p in range(PAIRS):
        block = sums[EARLY + 384 * p : EARLY + 384 * p + 384, :].astype(F32)
        for b in range(3):
            w_qkv[:, 384 * b + 128 * p : 384 * b + 128 * p + 128] = block[:, 128 * b : 128 * b + 128]
    g_attn[...] = sums[EARLY + 1152 : EARLY + 1168, :].astype(F32)[0:1].reshape(-1)
    mine = lax.axis_index("frame") // half
    far = far_tok[...].astype(F32)
    near = own_tok[...]
    d_tokens[mine] = near[0:cells]
    d_tokens[1 - mine] = far[0:cells]
    learned[mine] = near[cells : cells + MAPS]
    learned[1 - mine] = far[cells : cells + MAPS]


def vspec(n):
    return [pl.BlockSpec(memory_space=VMEM)] * n


def params(collective=None, mib=56):
    if collective is None:
        return pltpu.CompilerParams(vmem_limit_bytes=mib * MIB)
    return pltpu.CompilerParams(collective_id=collective, has_side_effects=True, vmem_limit_bytes=mib * MIB)


def tap_masks():
    p = np.arange(WIDE) % 256
    px, py = p // GRID, p % GRID
    out = np.zeros((16, WIDE), np.float32)
    for t in range(9):
        r, c = t // 3 - 1, t % 3 - 1
        out[t] = (p < CELLS) & (px + r >= 0) & (px + r < GRID) & (py + c >= 0) & (py + c < GRID)
    return out


def head_sums():
    out = np.zeros((HEADS * HEAD_DIM, 128), np.float32)
    for h in range(HEADS):
        out[h * HEAD_DIM : (h + 1) * HEAD_DIM, DEL0 + 3 * h : DEL0 + 3 * h + 3] = 1.0
    return out


def on_device(frames, seqs, tokens, segments, g_attn, w_qkv, w_out, g_mlp, w_up, w_down, g_learn, conv_first, conv_rest, d_learned):
    _, cells, width = tokens.shape
    rows = -(-(cells + 1 + MAPS) // 16) * 16
    own = 2 * rows
    total = frames * rows
    n_sems = 1 + 8 * frames
    sds = jax.ShapeDtypeStruct
    first9 = conv_first.transpose(1, 2, 0, 3).reshape(9, MAPS, width).astype(F32)
    rest27 = conv_rest.transpose(0, 2, 3, 1, 4).reshape(27, MAPS, MAPS).astype(F32)
    n_all = EARLY + LATE
    sizes = [landing(n, early_groups(frames, seqs), EARLY_BITS) for _, n in EARLY_CUTS]
    sizes += [landing(n, late_groups(frames, seqs), LATE_BITS) for _, n in LATE_CUTS]
    land_n, copies = (sum(v) for v in zip(*sizes))
    anywhere = pl.BlockSpec(memory_space=pl.ANY)
    sums, own_tok, far_tok = pl.pallas_call(
        functools.partial(whole_kernel, frames, seqs, rows, cells),
        out_shape=[sds((n_all, width), BF16), sds((rows, width), F32), sds((rows, width), BF16)],
        in_specs=vspec(14),
        out_specs=[anywhere] + vspec(2),
        scratch_shapes=[
            VMEM((2, rows, width), BF16),
            VMEM((frames, rows, width), BF16),
            VMEM((9, total, 128), BF16),
            VMEM((total, 128), BF16),
            VMEM((PAIRS + 1, total, 128), BF16),
            VMEM((PAIRS + 1, own, 128), BF16),
            VMEM((own, width), F32),
            VMEM((2, MAPS, width), F32),
            VMEM((own, 128), F32),
            VMEM((PAIRS, own, 128), F32),
            VMEM((own, width), F32),
            VMEM((own, width), F32),
            VMEM((own, width), F32),
            VMEM((own, width), F32),
            VMEM((own, 128), F32),
            VMEM((own, 128), F32),
            VMEM((own, width), F32),
            VMEM((4, own, width), F32),
            VMEM((WIDE, width), BF16),
            VMEM((WIDE, width), F32),
            VMEM((WIDE, width), F32),
            VMEM((80, width), BF16),
            VMEM((80, WIDE), BF16),
            VMEM((32, width), F32),
            VMEM((8, width), F32),
            VMEM((3, 80, 128), F32),
            VMEM((3, 16, 128), F32),
            VMEM((PAIRS, own, 128), BF16),
            VMEM((own, width), BF16),
            VMEM((own, width), F32),
            VMEM((n_all, width), BF16),
            VMEM((land_n, width), BF16),
            VMEM((n_all, width), BF16),
            VMEM((rows, width), BF16),
            VMEM((rows, width), BF16),
            pltpu.SemaphoreType.DMA((n_sems,)),
            pltpu.SemaphoreType.DMA((frames,)),
            pltpu.SemaphoreType.DMA((n_sems,)),
            pltpu.SemaphoreType.DMA((frames,)),
            pltpu.SemaphoreType.DMA((copies,)),
            pltpu.SemaphoreType.DMA((copies,)),
            pltpu.SemaphoreType.DMA((2,)),
            pltpu.SemaphoreType.DMA((2,)),
        ],
        compiler_params=params(0, 60),
        name="layer",
    )(
        jnp.pad(tokens, ((0, 0), (0, rows - cells), (0, 0))), segments, d_learned.astype(F32),
        g_attn, w_qkv, w_out, g_mlp, w_up, w_down, g_learn, first9, rest27,
        jnp.asarray(tap_masks()), jnp.asarray(head_sums()),
    )
    d_tokens, learned_all, dg_attn, d_w_qkv, d_w_out, dg_mlp, d_w_up, d_w_down, dg_learn, first, rest = pl.pallas_call(
        functools.partial(finish_kernel, cells, frames // 2),
        out_shape=[
            sds((2, cells, width), F32),
            sds((2, MAPS, width), F32),
            sds((width,), F32),
            sds((width, 3 * width), F32),
            sds((width, width), F32),
            sds((width,), F32),
            sds((width, 4 * width), F32),
            sds((4 * width, width), F32),
            sds((width,), F32),
            sds((72, width), F32),
            sds((24, 128), F32),
        ],
        in_specs=vspec(3),
        out_specs=vspec(11),
        compiler_params=params(),
        name="outputs",
    )(sums, own_tok, far_tok)
    d_first = first.reshape(3, 3, MAPS, width).transpose(2, 0, 1, 3)
    d_rest = rest[:, :72].reshape(3, MAPS, 3, 3, MAPS)
    return (
        learned_all.astype(BF16), d_tokens, dg_attn, d_w_qkv, d_w_out, dg_mlp, d_w_up, d_w_down, dg_learn, d_first, d_rest,
    )


def solution(mesh):
    frames, seqs = mesh.shape["frame"], mesh.shape["seq"]
    both = P("seq", "frame", None)
    in_specs = (both, P("seq", "frame"), *([P()] * 9), both)
    out_specs = (both, both, *([P()] * 9))
    return jax.shard_map(
        functools.partial(on_device, frames, seqs),
        mesh=mesh,
        in_specs=in_specs,
        out_specs=out_specs,
        check_vma=False,
    )
```

time: 198 us -> 174 us (0.88)
  Pallas kernels: 186 us -> 162 us
    pallas_call x3 -> x1, Pallas kernels: 181 us -> 156 us  [on_device(): pl.pallas_call(functools.partial(whole_kernel, frames, seqs, rows, cells)...]
where the time goes in v3:
time: 174 us; the launch traced here: 173 us
  Pallas kernels  162 us (93%)
  other arithmetic  5.59 us (3%)
  local copies, waits for them, and re-layouts  5.44 us (3%)
    pallas_call x1, Pallas kernels, on_device(): pl.pallas_call(functools.partial(whole_kernel, frames, seqs, rows, cells)...  156 us
    pallas_call x1, Pallas kernels, on_device(): pl.pallas_call(functools.partial(finish_kernel, cells, frames // 2), out_...  5.55 us
    unnamed x3, local copies, waits for them, and re-layouts  3.85 us

profile of v3, /device:TPU:0, one launch (start us, length us, event | category | flops | bytes accessed | tf_op | source)
XLA Modules:
  0.0 173.4 jit_solution(7598200788741810472)
XLA Ops:
  0.6 1.3 convert_element_type.22.d_learned
  2.0 1.5 convert_element_type.32
  3.4 1.5 convert_element_type.33
  4.9 1.0 copy.28
  5.9 0.8 pad.4.tokens
  6.7 156.2 %layer.1 = (bf16[4864,384]{1,0:T(8,128)(2,1)}, f32[208,384]{1,0:T(8,128)}, bf16[208,384]{1,0:T(8,128)(2,1)}) custom-call(bf16[2,208,384]{2,1,0:T(8,128)(2,1)} %pad.4.tokens, s32[2,196]{1,0:T(2,128)} %segments.1, f32[2,8,384]{2,1,0:T(8,128)} %convert_element_type.22.d_learned, f32[384]{0:T(512)} %g_attn.1, bf16[384,1152]{1,0:T(8,128)(2,1)} %w_qkv.1, ...), custom_call_target="tpu_custom_call" | custom-call | tf_op jit(solution)/shard_map/layer/pallas_call | solution.py:845
  162.8 5.5 %outputs.1 = (f32[2,196,384]{2,1,0:T(8,128)}, f32[2,8,384]{2,1,0:T(8,128)}, f32[384]{0:T(512)}, f32[384,1152]{1,0:T(8,128)}, f32[384,384]{1,0:T(8,128)}, /*index...) custom-call(bf16[4864,384]{1,0:T(8,128)(2,1)} %get-tuple-element.25., ...), custom_call_target="tpu_custom_call" | custom-call | tf_op jit(solution)/shard_map/outputs/pallas_call | solution.py:902
  168.4 1.3 convert_element_type.29
  169.7 0.8 reshape.35
  170.6 0.7 copy.30
  171.2 2.2 %copy.29 = f32[2,196,384]{2,0,1:T(2,128)} copy(f32[2,196,384]{2,1,0:T(8,128)} %get-tuple-element.51) | data formatting | bytes 1204224

commit v4 on v3

--- a/solution.py
+++ b/solution.py
@@ -95,7 +95,8 @@
 
 
 class Gather:
-    def __init__(self, half, base, turn, block, send, recv, first, fi, si):
+    def __init__(self, half, base, turn, block, send, recv, first, fi, si, shift=0):
+        self.shift = shift
         self.g, self.base, self.block, self.send, self.recv = fi % half, base, block, send, recv
         self.fi, self.si = fi, si
         bits = []
@@ -131,9 +132,15 @@
             at = at + ((j // (1 << k)) % 2) * self.delta(bit)
         return at + self.delta(1 if stage == self.last else self.order[stage - 1])
 
+    def nearby(self, j, core):
+        at = self.base + self.g
+        for k, bit in enumerate(self.order):
+            at = at + ((j // (1 << k)) % 2) * self.delta(bit)
+        return at + self.delta(1) if core else at
+
     def copy(self, slot, k, bit):
         ref = self.block(slot)
-        return rc(ref, ref, self.send.at[k], self.recv.at[slot], (flip(self.fi, bit), self.si))
+        return rc(ref, ref, self.send.at[k], self.recv.at[slot + self.shift], (flip(self.fi, bit), self.si))
 
     def run(self, stage):
         if stage > 0:
@@ -214,6 +221,7 @@
 
 
 TILE = 16
+UNROLL = 2
 
 
 def at_tile(start, n):
@@ -241,7 +249,7 @@
 EARLY = 3584
 LATE = 3 * 384 + 128
 EARLY_CUTS = ((0, 1536), (1536, 2048))
-LATE_CUTS = ((EARLY, 384), (EARLY + 384, 384), (EARLY + 768, 512))
+LATE_CUTS = ((EARLY, 384, 0), (EARLY + 384, 384, 1), (EARLY + 768, 512, 2))
 EARLY_BITS = 5
 LATE_BITS = 3
 
@@ -360,14 +368,14 @@
 
 def whole_kernel(
     frames, seqs, rows, cells,
-    tokens, segments, d_learned, g_attn, w_qkv, w_out, g_mlp, w_up, w_down, g_learn, first9, rest27, tapmask, blockones,
+    tokens, segments, small_in, g_attn, w_qkv, w_out_hbm, g_mlp, w_up_hbm, w_down_hbm, g_learn, tapmask, blockones,
     sums, own_tok, far_tok,
     xp, xg, qkv, augk, dag, da_ext, dx2_scr, learned,
-    augq, o_scr, x2_scr, y_scr, vhat2_scr, vhat3_scr, rstd2_scr, rstd3_scr,
+    augq, o_scr, x2_scr, y_scr, vhat2_scr, vhat3_scr, rstd_scr,
     dh2_scr, u_scr, h3p, yp,
     dyp, w72_scr, spread_scr, rest_scr, gain_scr, conv_bw, conv_fw, dqkv,
     h1_scr, dh1_scr, buf, land, out, tok_send, tok_land, tsend,
-    trecv, gsend, grecv, psend, precv, fsem, tsem,
+    trecv, gsend, grecv, psend, precv, fsem, tsem, wsem, w_out, w_up, w_down,
 ):
     fi = lax.axis_index("frame")
     si = lax.axis_index("seq")
@@ -378,21 +386,33 @@
     own = 2 * rows
     other = fi + half * (1 - 2 * mine)
     partner = (other, si)
+    weights = [
+        pltpu.make_async_copy(src, dst, wsem.at[i])
+        for i, (src, dst) in enumerate(((w_out_hbm, w_out), (w_up_hbm, w_up), (w_down_hbm, w_down)))
+    ]
+    for cp in weights:
+        cp.start()
     for k in range(2):
         body = tokens[k].astype(F32)[0:cells]
         seg = jnp.broadcast_to(segments[k : k + 1, 0:1].astype(F32), (1, 384))
         pad = jnp.zeros((rows - cells - 1 - MAPS, 384), F32)
-        xp[k] = jnp.concatenate([body, seg, d_learned[k], pad], axis=0).astype(BF16)
+        xp[k] = jnp.concatenate([body, seg, small_in[72 + MAPS * k : 72 + MAPS * (k + 1), :], pad], axis=0).astype(BF16)
     xg[fi] = xp[mine]
     singles = [[bit] for bit in mesh_bits(frames, seqs)]
     by_early, by_late = early_groups(frames, seqs), late_groups(frames, seqs)
-    greet(partners_of((singles, by_early, by_late), fi, si))
-    token_block = lambda slot: xg.at[slot]
-    near = Gather(half, half * mine, 0, token_block, tsend, trecv, 1, fi, si)
-    far = Gather(half, half * (1 - mine), 1, token_block, tsend, trecv, near.end, fi, si)
-    to_partner = rc(xp.at[1 - mine], xg.at[fi], tsend.at[0], trecv.at[fi], partner)
-    to_partner.start()
-    near.run(0)
+    greet(partners_of((singles + [[("frame", 1)]],), fi, si))
+    cut = (rows // 2 + 15) // 16 * 16
+    near, far, to_partner = [], [], []
+    end = 2
+    for n, span in enumerate((pl.ds(0, cut), pl.ds(cut, rows - cut))):
+        to_partner.append(rc(xp.at[1 - mine, span, :], xg.at[fi, span, :], tsend.at[n], trecv.at[fi + n * frames], partner))
+        to_partner[n].start()
+        block = lambda slot, span=span: xg.at[slot, span, :]
+        for group, base in ((near, half * mine), (far, half * (1 - mine))):
+            group.append(Gather(half, base, n, block, tsend, trecv, end, fi, si, n * frames))
+            end = group[-1].end
+    for piece in near:
+        piece.run(0)
     da_block = lambda slot: dag.at[:, pl.ds(pl.multiple_of(slot * rows, rows), rows), :]
     da_near = Gather(half, 0, 0, da_block, gsend, grecv, 0, fi, si)
     da_far = Gather(half, half, 1, da_block, gsend, grecv, da_near.end, fi, si)
@@ -400,7 +420,7 @@
     early, late = [], []
     land_at = sem_at = 0
     for group, cuts, by, bits in ((early, EARLY_CUTS, by_early, EARLY_BITS), (late, LATE_CUTS, by_late, LATE_BITS)):
-        for start, length in cuts:
+        for start, length, *_ in cuts:
             group.append(Piece(start, length, by, bits, land_at, sem_at, *refs))
             land_at, sem_at = group[-1].land_end, group[-1].sem_end
 
@@ -417,14 +437,12 @@
     row128 = iota((rows, 128), 0)
     valid_row = row128 < cells
 
-    w72 = first9[...].reshape(72, 384)
-    w72_scr[...] = sixteen(w72).astype(BF16)
+    w72_scr[...] = sixteen(small_in[0:72, :]).astype(BF16)
     square_r, square_c = iota((128, 128), 0), iota((128, 128), 1)
     repeat = ((square_c & 7) == square_r).astype(F32)
     same_tap = (((square_r >> 3) == (square_c >> 3)) & (square_r < 72)).astype(F32)
     for layer in range(3):
-        by_tap = rest27[9 * layer : 9 * layer + 9].reshape(72, MAPS)
-        by_tap = jnp.concatenate([by_tap, jnp.zeros((72, 120), F32)], axis=1)
+        by_tap = small_in[88 + 72 * layer : 160 + 72 * layer, 0:128]
         conv_bw[layer] = sixteen(by_tap)
         by_tap = jnp.concatenate([by_tap, jnp.zeros((56, 128), F32)], axis=0)
         conv_fw[layer] = nn(repeat[0:16], nn(by_tap, repeat, HIGH) * same_tap, HIGH)
@@ -448,27 +466,41 @@
         ).astype(BF16)
         return carry
 
-    def project_stage(gather, stage):
-        gather.run(stage)
-        if stage == 0:
-            project(gather.slot(0, 0), 0)
-        else:
-            lax.fori_loop(0, gather.arrivals(stage), lambda j, c: project(gather.slot(stage, j), c), 0)
-
-    project(near.slot(0, 0), 0)
-    project_stage(near, 1)
-    far_block = xg.at[other]
-    rc(far_block, far_block, tsend.at[0], trecv.at[other], partner).wait_recv()
-    project_stage(far, 0)
-    for stage in range(2, near.last):
-        project_stage(near, stage)
-    for stage in range(1, near.last):
-        project_stage(far, stage)
-    project_stage(near, near.last)
-    project_stage(far, far.last)
-    to_partner.wait_send()
-    near.drain()
-    far.drain()
+    def run(gather, stage):
+        for piece in gather:
+            piece.run(stage)
+
+    def project_range(gather, start, core):
+        n = 1 << gather[0].n
+
+        def one(j, carry):
+            return project(gather[0].nearby(j, core), carry)
+
+        lax.fori_loop(start, n, one, 0, unroll=min(n - start, UNROLL))
+
+    last = near[0].last
+    project(fi, 0)
+    run(near, 1)
+    for n, piece in enumerate(far):
+        here = piece.block(other)
+        rc(here, here, tsend.at[0], trecv.at[other + n * frames], partner).wait_recv()
+        piece.run(0)
+    project(other, 0)
+    for stage in range(2, last):
+        run(near, stage)
+    for stage in range(1, last):
+        run(far, stage)
+        if stage == 1:
+            project_range(near, 1, False)
+    run(near, last)
+    project_range(far, 1, False)
+    project_range(near, 0, True)
+    run(far, last)
+    project_range(far, 0, True)
+    for cp in to_partner:
+        cp.wait_send()
+    for piece in near + far:
+        piece.drain()
 
     ones = jnp.ones((frames * rows, 128), BF16)
 
@@ -509,6 +541,9 @@
 
     lax.fori_loop(0, 4 * PAIRS // together, attend, 0)
 
+    for cp in weights:
+        cp.wait()
+
     def apart(fn):
         pl.when(fi >= 0)(fn)
 
@@ -523,7 +558,7 @@
         x2_scr[...] = x2
         y_scr[...] = x2
         vhat, rstd = normed(x2)
-        rstd2_scr[...] = jnp.broadcast_to(rstd, (own, 128))
+        rstd_scr[...] = jnp.broadcast_to(rstd, (own, 128))
         vhat2_scr[...] = vhat
         out[h2_rows, :] = (vhat * g_mlp[...].reshape(1, -1)).astype(BF16)
 
@@ -543,7 +578,7 @@
         y = y_scr[...]
         vhat, rstd = normed(y)
         vhat3_scr[...] = vhat
-        rstd3_scr[...] = jnp.broadcast_to(rstd, (own, 128))
+        rstd_scr[...] = jnp.where(iota((own, 128), 1) < 64, rstd_scr[...], rstd)
         h3 = (vhat * g_learn[...].reshape(1, -1)).astype(BF16)
         for k in range(2):
             yp[256 * k : 256 * k + rows, :] = y[k * rows : (k + 1) * rows, :]
@@ -604,7 +639,7 @@
     def _():
         dh3 = tn(spread_scr[...], w72_scr[...])
         dh3 = jnp.concatenate([dh3[0:rows], dh3[256 : 256 + rows]], axis=0)
-        dy, dg3 = norm_back(vhat3_scr[...], rstd3_scr[:, 0:1], dh3, g_learn[...].reshape(1, -1))
+        dy, dg3 = norm_back(vhat3_scr[...], rstd_scr[:, 64:65], dh3, g_learn[...].reshape(1, -1))
         dy = dy + jnp.concatenate([dyp[0:rows, :], dyp[256 : 256 + rows, :]], axis=0)
         y_scr[...] = dy
         out[dm_rows, :] = dy.astype(BF16)
@@ -625,7 +660,7 @@
 
     @apart
     def _():
-        dx2, dg2 = norm_back(vhat2_scr[...], rstd2_scr[:, 0:1], dh2_scr[...], g_mlp[...].reshape(1, -1))
+        dx2, dg2 = norm_back(vhat2_scr[...], rstd_scr[:, 0:1], dh2_scr[...], g_mlp[...].reshape(1, -1))
         dx2 = dx2 + y_scr[...]
         dx2_scr[...] = dx2
         out[dm_rows, :] = dx2.astype(BF16)
@@ -714,10 +749,11 @@
 
                 def point(i=i, k=k):
                     early_point(i)
-                    for m in range(k):
-                        step = 2 * (k - m - 1) + j
-                        late[m].finish(step)
-                        late[m].start(step + 1)
+                    for piece, (_, _, after) in zip(late, LATE_CUTS):
+                        if after < k:
+                            step = 2 * (k - after - 1) + j
+                            piece.finish(step)
+                            piece.start(step + 1)
 
                 pl.when(p == k)(point)
 
@@ -732,14 +768,17 @@
             [w_qkv[:, pl.ds(pl.multiple_of(384 * b + 128 * p, 128), 128)] for b in range(3)], axis=1
         )
         dh1_scr[...] += nt(d, w)
-        for k in range(PAIRS - 1):
-            pl.when(p == k)(lambda k=k: late[k].start(0))
+        for piece, (_, _, after) in zip(late, LATE_CUTS):
+            if after < PAIRS - 1:
+                pl.when(p == after)(functools.partial(piece.start, 0))
         return carry
 
     lax.fori_loop(0, PAIRS, key_pass, 0)
     dx, dg = norm_back(*normed(x), dh1_scr[...], g_attn[...].reshape(1, -1))
     buf[EARLY + 1152 : EARLY + 1168, :] = jnp.concatenate([dg, jnp.zeros((15, 384), F32)], axis=0).astype(BF16)
-    late[2].start(0)
+    for piece, (_, _, after) in zip(late, LATE_CUTS):
+        if after == PAIRS - 1:
+            piece.start(0)
     dx = dx + dx2_scr[...]
     for k in range(2):
         tail = jnp.concatenate([learned[k], jnp.zeros((rows - cells - MAPS, 384), F32)], axis=0)
@@ -760,7 +799,7 @@
         for i, (at, n) in enumerate((EARLY_CUTS[0], (EARLY_CUTS[1][0], EARLY + LATE - EARLY_CUTS[1][0])))
     ]
     running = [(piece, 1 + len(points)) for piece, points in zip(early, EARLY_POINTS)]
-    running += [(piece, 2 * (PAIRS - 1 - m)) for m, piece in enumerate(late)]
+    running += [(piece, 2 * (PAIRS - 1 - after)) for piece, (_, _, after) in zip(late, LATE_CUTS)]
     for piece, n in running[:1]:
         for i in range(n, piece.total):
             piece.finish(i)
@@ -783,8 +822,10 @@
     w_down[...] = sums[1536:3072, :].astype(F32)
     w_out[...] = sums[3072:3456, :].astype(F32)
     small = sums[3456:3584, :].astype(F32)
-    first[...] = small[0:72]
-    rest[...] = small[80:104, 0:128]
+    first[...] = small[0:72].reshape(9, MAPS, 384)
+    for n in range(27):
+        layer, t = n // 9, n % 9
+        rest[n] = small[80 + MAPS * layer : 88 + MAPS * layer, MAPS * t : MAPS * (t + 1)]
     g_mlp[...] = small[72:73].reshape(-1)
     g_learn[...] = small[73:74].reshape(-1)
     for p in range(PAIRS):
@@ -797,8 +838,8 @@
     near = own_tok[...]
     d_tokens[mine] = near[0:cells]
     d_tokens[1 - mine] = far[0:cells]
-    learned[mine] = near[cells : cells + MAPS]
-    learned[1 - mine] = far[cells : cells + MAPS]
+    a, b = near[cells : cells + MAPS], far[cells : cells + MAPS]
+    learned[...] = jnp.where(mine == 0, jnp.concatenate([a, b], axis=0), jnp.concatenate([b, a], axis=0)).astype(BF16)
 
 
 def vspec(n):
@@ -833,19 +874,26 @@
     rows = -(-(cells + 1 + MAPS) // 16) * 16
     own = 2 * rows
     total = frames * rows
-    n_sems = 1 + 8 * frames
+    n_sems = 2 + 16 * frames
     sds = jax.ShapeDtypeStruct
-    first9 = conv_first.transpose(1, 2, 0, 3).reshape(9, MAPS, width).astype(F32)
-    rest27 = conv_rest.transpose(0, 2, 3, 1, 4).reshape(27, MAPS, MAPS).astype(F32)
+    rest = conv_rest.transpose(0, 2, 3, 1, 4).reshape(27 * MAPS, MAPS)
+    small_in = jnp.concatenate(
+        [
+            conv_first.transpose(1, 2, 0, 3).reshape(9 * MAPS, width),
+            d_learned.reshape(2 * MAPS, width),
+            jnp.pad(rest, ((0, 0), (0, width - MAPS))),
+        ],
+        axis=0,
+    ).astype(F32)
     n_all = EARLY + LATE
     sizes = [landing(n, early_groups(frames, seqs), EARLY_BITS) for _, n in EARLY_CUTS]
-    sizes += [landing(n, late_groups(frames, seqs), LATE_BITS) for _, n in LATE_CUTS]
+    sizes += [landing(n, late_groups(frames, seqs), LATE_BITS) for _, n, _ in LATE_CUTS]
     land_n, copies = (sum(v) for v in zip(*sizes))
     anywhere = pl.BlockSpec(memory_space=pl.ANY)
     sums, own_tok, far_tok = pl.pallas_call(
         functools.partial(whole_kernel, frames, seqs, rows, cells),
         out_shape=[sds((n_all, width), BF16), sds((rows, width), F32), sds((rows, width), BF16)],
-        in_specs=vspec(14),
+        in_specs=vspec(5) + [anywhere] + vspec(1) + [anywhere] * 2 + vspec(3),
         out_specs=[anywhere] + vspec(2),
         scratch_shapes=[
             VMEM((2, rows, width), BF16),
@@ -862,7 +910,6 @@
             VMEM((own, width), F32),
             VMEM((own, width), F32),
             VMEM((own, width), F32),
-            VMEM((own, 128), F32),
             VMEM((own, 128), F32),
             VMEM((own, width), F32),
             VMEM((4, own, width), F32),
@@ -884,26 +931,30 @@
             VMEM((rows, width), BF16),
             VMEM((rows, width), BF16),
             pltpu.SemaphoreType.DMA((n_sems,)),
-            pltpu.SemaphoreType.DMA((frames,)),
+            pltpu.SemaphoreType.DMA((2 * frames,)),
             pltpu.SemaphoreType.DMA((n_sems,)),
             pltpu.SemaphoreType.DMA((frames,)),
             pltpu.SemaphoreType.DMA((copies,)),
             pltpu.SemaphoreType.DMA((copies,)),
             pltpu.SemaphoreType.DMA((2,)),
             pltpu.SemaphoreType.DMA((2,)),
+            pltpu.SemaphoreType.DMA((3,)),
+            VMEM((width, width), BF16),
+            VMEM((width, 4 * width), BF16),
+            VMEM((4 * width, width), BF16),
         ],
-        compiler_params=params(0, 60),
+        compiler_params=params(0, 61),
         name="layer",
     )(
-        jnp.pad(tokens, ((0, 0), (0, rows - cells), (0, 0))), segments, d_learned.astype(F32),
-        g_attn, w_qkv, w_out, g_mlp, w_up, w_down, g_learn, first9, rest27,
+        jnp.pad(tokens, ((0, 0), (0, rows - cells), (0, 0))), segments, small_in,
+        g_attn, w_qkv, w_out, g_mlp, w_up, w_down, g_learn,
         jnp.asarray(tap_masks()), jnp.asarray(head_sums()),
     )
     d_tokens, learned_all, dg_attn, d_w_qkv, d_w_out, dg_mlp, d_w_up, d_w_down, dg_learn, first, rest = pl.pallas_call(
         functools.partial(finish_kernel, cells, frames // 2),
         out_shape=[
             sds((2, cells, width), F32),
-            sds((2, MAPS, width), F32),
+            sds((2 * MAPS, width), BF16),
             sds((width,), F32),
             sds((width, 3 * width), F32),
             sds((width, width), F32),
@@ -911,8 +962,8 @@
             sds((width, 4 * width), F32),
             sds((4 * width, width), F32),
             sds((width,), F32),
-            sds((72, width), F32),
-            sds((24, 128), F32),
+            sds((9, MAPS, width), F32),
+            sds((27, MAPS, MAPS), F32),
         ],
         in_specs=vspec(3),
         out_specs=vspec(11),
@@ -920,9 +971,9 @@
         name="outputs",
     )(sums, own_tok, far_tok)
     d_first = first.reshape(3, 3, MAPS, width).transpose(2, 0, 1, 3)
-    d_rest = rest[:, :72].reshape(3, MAPS, 3, 3, MAPS)
+    d_rest = rest.reshape(3, 3, 3, MAPS, MAPS).transpose(0, 3, 1, 2, 4)
     return (
-        learned_all.astype(BF16), d_tokens, dg_attn, d_w_qkv, d_w_out, dg_mlp, d_w_up, d_w_down, dg_learn, d_first, d_rest,
+        learned_all.reshape(2, MAPS, width), d_tokens, dg_attn, d_w_qkv, d_w_out, dg_mlp, d_w_up, d_w_down, dg_learn, d_first, d_rest,
     )
 
 

time: 174 us -> 166 us (0.954)
  other arithmetic: 5.59 us -> 1.66 us
  Pallas kernels: 162 us -> 159 us
    convert_element_type x4 -> x1, other arithmetic: 5.59 us -> 1.66 us  [on_device(): small_in = jnp.concatenate([conv_first.transpose(1, 2, 0, 3).reshape(9 *...]
    pallas_call x1, Pallas kernels: 156 us -> 154 us  [on_device(): pl.pallas_call(functools.partial(whole_kernel, frames, seqs, rows, cells)...]
    unnamed x3 -> x2, local copies, waits for them, and re-layouts: 3.85 us -> 3.2 us
where the time goes in v4:
time: 166 us; the launch traced here: 165 us
  Pallas kernels  159 us (96%)
  local copies, waits for them, and re-layouts  3.96 us (2%)
    pallas_call x1, Pallas kernels, on_device(): pl.pallas_call(functools.partial(whole_kernel, frames, seqs, rows, cells)...  154 us
    pallas_call x1, Pallas kernels, on_device(): pl.pallas_call(functools.partial(finish_kernel, cells, frames // 2), out_...  5.43 us

profile of v4, /device:TPU:0, one launch (start us, length us, event | category | flops | bytes accessed | tf_op | source)
XLA Modules:
  0.0 165.5 jit_solution(14359210076567762504)
XLA Ops:
  0.6 1.0 copy.25
  1.6 0.8 pad.8.tokens
  2.4 1.7 %fusion.2.small_in = f32[304,384]{1,0:T(8,128)} fusion(bf16[216,8]{1,0:T(8,128)(2,1)} %bitcast.14, bf16[16,384]{1,0:T(8,128)(2,1)} %bitcast.16, bf16[72,384]{1,0:T(8,128)(2,1)} %bitcast.15), kind=kLoop, calls=%fused_computation.3 | loop fusion | flops 933888 | bytes 537984 | tf_op jit(solution)/shard_map/convert_element_type | solution.py:887
  4.1 153.8 %layer.1 = (bf16[4864,384]{1,0:T(8,128)(2,1)}, f32[208,384]{1,0:T(8,128)}, bf16[208,384]{1,0:T(8,128)(2,1)}) custom-call(bf16[2,208,384]{2,1,0:T(8,128)(2,1)} %pad.8.tokens, s32[2,196]{1,0:T(2,128)} %segments.1, f32[304,384]{1,0:T(8,128)} %fusion.2.small_in, f32[384]{0:T(512)} %g_attn.1, bf16[384,1152]{1,0:T(8,128)(2,1)} %w_qkv.1, ...), custom_call_target="tpu_custom_call" | custom-call | tf_op jit(solution)/shard_map/layer/pallas_call | solution.py:893
  157.8 5.4 %outputs.1 = (f32[2,196,384]{2,1,0:T(8,128)}, bf16[16,384]{1,0:T(8,128)(2,1)}, f32[384]{0:T(512)}, f32[384,1152]{1,0:T(8,128)}, f32[384,384]{1,0:T(8,128)}, /*in...) custom-call(bf16[4864,384]{1,0:T(8,128)(2,1)} %get-tuple-element.25., ...), custom_call_target="tpu_custom_call" | custom-call | tf_op jit(solution)/shard_map/outputs/pallas_call | solution.py:953
  163.3 2.2 %copy.26 = f32[2,196,384]{2,0,1:T(2,128)} copy(f32[2,196,384]{2,1,0:T(8,128)} %get-tuple-element.40) | data formatting | bytes 1204224

commit v5 on v4

--- a/solution.py
+++ b/solution.py
@@ -221,7 +221,7 @@
 
 
 TILE = 16
-UNROLL = 2
+UNROLL = 4
 
 
 def at_tile(start, n):
@@ -249,7 +249,7 @@
 EARLY = 3584
 LATE = 3 * 384 + 128
 EARLY_CUTS = ((0, 1536), (1536, 2048))
-LATE_CUTS = ((EARLY, 384, 0), (EARLY + 384, 384, 1), (EARLY + 768, 512, 2))
+LATE_CUTS = ((EARLY, 1280, 2),)
 EARLY_BITS = 5
 LATE_BITS = 3
 
@@ -363,7 +363,7 @@
     return devs
 
 
-EARLY_POINTS = ((2, 5, 6, 7, 8, 10, 11), (4, 6, 7, 8, 9))
+EARLY_POINTS = ((3, 6, 7, 8, 9, 11), (5, 7, 8, 9, 10))
 
 
 def whole_kernel(
@@ -669,9 +669,6 @@
         small = [d_first, gains, rest_scr[...], jnp.zeros((16, 384), F32)]
         buf[3456:3584, :] = jnp.concatenate(small, axis=0).astype(BF16)
 
-    early[0].finish(0)
-    early[0].start(1)
-
     @apart
     def _():
         dzz = out[dm_rows, :]
@@ -691,6 +688,8 @@
             there = pl.ds(pl.multiple_of((g + half * k) * rows, rows), rows)
             dag[:, there, :] = da_ext[:, k * rows : (k + 1) * rows, :]
 
+    early[0].finish(0)
+    early[0].start(1)
     early[1].start(0)
     da_near.run(0)
     da_far.run(0)

time: 166 us -> 157 us (0.946)
  Pallas kernels: 159 us -> 151 us
    pallas_call x1, Pallas kernels: 154 us -> 145 us  [on_device(): pl.pallas_call(functools.partial(whole_kernel, frames, seqs, rows, cells)...]
where the time goes in v5:
time: 157 us
  Pallas kernels  151 us (96%)
  local copies, waits for them, and re-layouts  3.96 us (3%)
  other arithmetic  1.66 us (1%)
    pallas_call x1, Pallas kernels, on_device(): pl.pallas_call(functools.partial(whole_kernel, frames, seqs, rows, cells)...  145 us
    pallas_call x1, Pallas kernels, on_device(): pl.pallas_call(functools.partial(finish_kernel, cells, frames // 2), out_...  5.43 us
    unnamed x2, local copies, waits for them, and re-layouts  3.2 us

profile of v5, /device:TPU:0, one launch (start us, length us, event | category | flops | bytes accessed | tf_op | source)
XLA Modules:
  0.0 157.0 jit_solution(15107034144606275617)
XLA Ops:
  0.6 1.0 copy.25
  1.6 0.8 pad.8.tokens
  2.4 1.7 %fusion.2.small_in = f32[304,384]{1,0:T(8,128)} fusion(bf16[216,8]{1,0:T(8,128)(2,1)} %bitcast.14, bf16[16,384]{1,0:T(8,128)(2,1)} %bitcast.16, bf16[72,384]{1,0:T(8,128)(2,1)} %bitcast.15), kind=kLoop, calls=%fused_computation.3 | loop fusion | flops 933888 | bytes 537984 | tf_op jit(solution)/shard_map/convert_element_type | solution.py:886
  4.1 145.3 %layer.1 = (bf16[4864,384]{1,0:T(8,128)(2,1)}, f32[208,384]{1,0:T(8,128)}, bf16[208,384]{1,0:T(8,128)(2,1)}) custom-call(bf16[2,208,384]{2,1,0:T(8,128)(2,1)} %pad.8.tokens, s32[2,196]{1,0:T(2,128)} %segments.1, f32[304,384]{1,0:T(8,128)} %fusion.2.small_in, f32[384]{0:T(512)} %g_attn.1, bf16[384,1152]{1,0:T(8,128)(2,1)} %w_qkv.1, ...), custom_call_target="tpu_custom_call" | custom-call | tf_op jit(solution)/shard_map/layer/pallas_call | solution.py:892
  149.4 5.4 %outputs.1 = (f32[2,196,384]{2,1,0:T(8,128)}, bf16[16,384]{1,0:T(8,128)(2,1)}, f32[384]{0:T(512)}, f32[384,1152]{1,0:T(8,128)}, f32[384,384]{1,0:T(8,128)}, /*in...) custom-call(bf16[4864,384]{1,0:T(8,128)(2,1)} %get-tuple-element.25., ...), custom_call_target="tpu_custom_call" | custom-call | tf_op jit(solution)/shard_map/outputs/pallas_call | solution.py:952
  154.8 2.2 %copy.26 = f32[2,196,384]{2,0,1:T(2,128)} copy(f32[2,196,384]{2,1,0:T(8,128)} %get-tuple-element.40) | data formatting | bytes 1204224

commit v6 on v5

--- a/solution.py
+++ b/solution.py
@@ -249,7 +249,7 @@
 EARLY = 3584
 LATE = 3 * 384 + 128
 EARLY_CUTS = ((0, 1536), (1536, 2048))
-LATE_CUTS = ((EARLY, 1280, 2),)
+LATE_CUTS = ((EARLY, 1152, 2), (EARLY + 1152, 128, 2))
 EARLY_BITS = 5
 LATE_BITS = 3
 
@@ -712,7 +712,7 @@
     )
     chunk = 256
     pieces_n = total // chunk
-    split = (pieces_n + 1) // 2
+    split = pieces_n // 2 - 1
 
     def query_pass(p, carry):
         def at_point(j):
@@ -773,11 +773,10 @@
         return carry
 
     lax.fori_loop(0, PAIRS, key_pass, 0)
+    late[0].start(0)
     dx, dg = norm_back(*normed(x), dh1_scr[...], g_attn[...].reshape(1, -1))
     buf[EARLY + 1152 : EARLY + 1168, :] = jnp.concatenate([dg, jnp.zeros((15, 384), F32)], axis=0).astype(BF16)
-    for piece, (_, _, after) in zip(late, LATE_CUTS):
-        if after == PAIRS - 1:
-            piece.start(0)
+    late[1].start(0)
     dx = dx + dx2_scr[...]
     for k in range(2):
         tail = jnp.concatenate([learned[k], jnp.zeros((rows - cells - MAPS, 384), F32)], axis=0)
@@ -835,8 +834,9 @@
     mine = lax.axis_index("frame") // half
     far = far_tok[...].astype(F32)
     near = own_tok[...]
-    d_tokens[mine] = near[0:cells]
-    d_tokens[1 - mine] = far[0:cells]
+    a, b = near[0:cells], far[0:cells]
+    d_tokens[:, 0, :] = jnp.where(mine == 0, a, b)
+    d_tokens[:, 1, :] = jnp.where(mine == 0, b, a)
     a, b = near[cells : cells + MAPS], far[cells : cells + MAPS]
     learned[...] = jnp.where(mine == 0, jnp.concatenate([a, b], axis=0), jnp.concatenate([b, a], axis=0)).astype(BF16)
 
@@ -952,7 +952,7 @@
     d_tokens, learned_all, dg_attn, d_w_qkv, d_w_out, dg_mlp, d_w_up, d_w_down, dg_learn, first, rest = pl.pallas_call(
         functools.partial(finish_kernel, cells, frames // 2),
         out_shape=[
-            sds((2, cells, width), F32),
+            sds((cells, 2, width), F32),
             sds((2 * MAPS, width), BF16),
             sds((width,), F32),
             sds((width, 3 * width), F32),
@@ -972,7 +972,7 @@
     d_first = first.reshape(3, 3, MAPS, width).transpose(2, 0, 1, 3)
     d_rest = rest.reshape(3, 3, 3, MAPS, MAPS).transpose(0, 3, 1, 2, 4)
     return (
-        learned_all.reshape(2, MAPS, width), d_tokens, dg_attn, d_w_qkv, d_w_out, dg_mlp, d_w_up, d_w_down, dg_learn, d_first, d_rest,
+        learned_all.reshape(2, MAPS, width), d_tokens.transpose(1, 0, 2), dg_attn, d_w_qkv, d_w_out, dg_mlp, d_w_up, d_w_down, dg_learn, d_first, d_rest,
     )
 
 

time: 157 us -> 154 us (0.981)
  local copies, waits for them, and re-layouts: 3.96 us -> 1.76 us
  Pallas kernels: 151 us -> 149 us
    unnamed x2 -> x1, local copies, waits for them, and re-layouts: 3.2 us -> 1 us
    pallas_call x1, Pallas kernels: 145 us -> 144 us  [on_device(): pl.pallas_call(functools.partial(whole_kernel, frames, seqs, rows, cells)...]
where the time goes in v6:
time: 154 us; the launch traced here: 153 us
  Pallas kernels  149 us (97%)
  local copies, waits for them, and re-layouts  1.76 us (1%)
  other arithmetic  1.66 us (1%)
    pallas_call x1, Pallas kernels, on_device(): pl.pallas_call(functools.partial(whole_kernel, frames, seqs, rows, cells)...  144 us
    pallas_call x1, Pallas kernels, on_device(): pl.pallas_call(functools.partial(finish_kernel, cells, frames // 2), out_...  5.45 us

profile of v6, /device:TPU:0, one launch (start us, length us, event | category | flops | bytes accessed | tf_op | source)
XLA Modules:
  0.0 153.4 jit_solution(14070020778124409836)
XLA Ops:
  0.6 1.0 copy.25
  1.6 0.8 pad.8.tokens
  2.4 1.7 %fusion.2.small_in = f32[304,384]{1,0:T(8,128)} fusion(bf16[216,8]{1,0:T(8,128)(2,1)} %bitcast.15, bf16[16,384]{1,0:T(8,128)(2,1)} %bitcast.17, bf16[72,384]{1,0:T(8,128)(2,1)} %bitcast.16), kind=kLoop, calls=%fused_computation.3 | loop fusion | flops 933888 | bytes 537984 | tf_op jit(solution)/shard_map/convert_element_type | solution.py:886
  4.1 143.7 %layer.1 = (bf16[4864,384]{1,0:T(8,128)(2,1)}, f32[208,384]{1,0:T(8,128)}, bf16[208,384]{1,0:T(8,128)(2,1)}) custom-call(bf16[2,208,384]{2,1,0:T(8,128)(2,1)} %pad.8.tokens, s32[2,196]{1,0:T(2,128)} %segments.1, f32[304,384]{1,0:T(8,128)} %fusion.2.small_in, f32[384]{0:T(512)} %g_attn.1, bf16[384,1152]{1,0:T(8,128)(2,1)} %w_qkv.1, ...), custom_call_target="tpu_custom_call" | custom-call | tf_op jit(solution)/shard_map/layer/pallas_call | solution.py:892
  147.8 5.5 %outputs.1 = (f32[196,2,384]{2,1,0:T(2,128)}, bf16[16,384]{1,0:T(8,128)(2,1)}, f32[384]{0:T(512)}, f32[384,1152]{1,0:T(8,128)}, f32[384,384]{1,0:T(8,128)}, /*in...) custom-call(bf16[4864,384]{1,0:T(8,128)(2,1)} %get-tuple-element.25., ...), custom_call_target="tpu_custom_call" | custom-call | tf_op jit(solution)/shard_map/outputs/pallas_call | solution.py:952
